TPU v7x, 512 devices: a whole 4x8x8 slice. The times are simulated.
512 devices in a mesh: gx: 32 (over y_hi, x, core), gy: 16 (over y_lo, z).
Axes of the slice: x: 4, y: 8 (y_hi: 4, y_lo: 2; y = y_hi * 2 + y_lo), z: 8, core: 2. Of those that a mesh axis runs over, the one named last changes fastest.
Arguments:
- source: float32 [4, 512, 512, 128], P(None, 'gx', 'gy'), may hold values from -6 to 6
- conduct_fine: float32 [512, 512, 128], P('gx', 'gy'), may hold values from 0.05 to 0.3
- conduct_second: float32 [256, 256, 64], P('gx', 'gy'), may hold values from 0.05 to 0.3
- conduct_third: float32 [128, 128, 32], P('gx', 'gy'), may hold values from 0.05 to 0.3
- conduct_coarse: float32 [64, 64, 16], P('gx', 'gy'), may hold values from 0.05 to 0.3
- mixers: float32 [4, 4, 4], replicated, may hold values from -1.5 to 1.5
- smoothers: float32 [4, 4, 4], replicated, may hold values from -0.75 to 0.75
Outputs:
- solution: float32 [4, 512, 512, 128], P(None, 'gx', 'gy')
All inputs are finite; a program needn't handle non-finite values.
Results may differ from a plain program's by a relative error of at most 0.00011.
Values sent between devices are 32-bit elements; how exact they have to be, the bound alone decides.
A program may use at most 128 MiB of HBM per device.

v0:
```python
import functools
import math

import jax
import jax.numpy as jnp
from jax import lax
from jax.experimental import pallas as pl
from jax.experimental.pallas import tpu as pltpu
from jax.sharding import PartitionSpec as P

MESH = pl.DeviceIdType.MESH
F32 = jnp.float32
BF16 = jnp.bfloat16
LANES = 128
PAD = 8


def spread(field, matrix):
    high = field.astype(BF16)
    low = (field - high.astype(F32)).astype(BF16)
    return jnp.dot(high, matrix, preferred_element_type=F32) + jnp.dot(
        low, matrix, preferred_element_type=F32
    )


def lane_index(shape):
    return lax.broadcasted_iota(jnp.int32, shape, len(shape) - 1)


def beside_z(field, segment):
    lane = lane_index((1, LANES)) % segment
    axis = field.ndim - 1
    before = jnp.where(lane == 0, 0.0, pltpu.roll(field, 1, axis))
    after = jnp.where(lane == segment - 1, 0.0, pltpu.roll(field, LANES - 1, axis))
    return before + after


def stencil(center, beside, coefficient, segment):
    total = beside + beside_z(center, segment)
    return coefficient * (6.0 * center - total) + center


def kernel(
    nx, ny,
    source, fine, second, third, coarse, mixers, smoothers, out,
    f0, g0, v0, r0, q0, s0, p0, c0,
    a1, f1, g1, v1, r1, q1, w1, s1, p1, c1,
    a2, f2, g2, v2, r2, q2, w2, s2, p2, c2,
    a3, r3, g3, w3, b3, s3, p3, line, lines,
    table, down, up, last_down, last_up,
    send_sem, recv_sem, local_sem, out_sem,
):
    mx, my = lax.axis_index("gx"), lax.axis_index("gy")

    def device(dx, dy):
        return (lax.rem(mx + (dx + nx), nx), lax.rem(my + (dy + ny), ny))

    barrier = pltpu.get_barrier_semaphore()
    peers = [(0, k) for k in range(1, ny)]
    peers += [(dx, dy) for dx in (-1, 1) for dy in (-1, 0, 1)] + [(-2, 0), (2, 0)]
    for dx, dy in peers:
        pl.semaphore_signal(barrier, inc=1, device_id=device(dx, dy), device_id_type=MESH)

    x0, y0 = f0.shape[1:3]
    x1, y1 = f1.shape[1:3]
    x2, y2 = f2.shape[:2]
    x3, y3 = a3.shape[:2]
    loads = [
        pltpu.make_async_copy(source, f0, local_sem.at[0]),
        pltpu.make_async_copy(fine, g0.at[4, pl.ds(2, x0), pl.ds(PAD, y0)], local_sem.at[1]),
        pltpu.make_async_copy(second, a1, local_sem.at[2]),
        pltpu.make_async_copy(third, a2, local_sem.at[3]),
        pltpu.make_async_copy(coarse, a3, local_sem.at[4]),
    ]
    for load in loads:
        load.start()

    def smooth_matrix(level):
        return [
            [smoothers[level, i, j] + (0.25 if i == j else 0.0) for j in range(4)]
            for i in range(4)
        ]

    def mix_matrix(level):
        return [
            [mixers[level, i, j] + (1.0 if i == j else 0.0) for j in range(4)] for i in range(4)
        ]

    def product(left, right):
        return [
            [sum(left[i][k] * right[k][j] for k in range(4)) for j in range(4)] for i in range(4)
        ]

    lane = lane_index((1, LANES))
    rows_used = [0]

    def keep(vector):
        row = rows_used[0]
        rows_used[0] += 1
        table[row : row + 1, :] = vector
        return row

    def pair_rows(matrix):
        return [
            [
                [
                    keep(
                        jnp.where(
                            lane < 64,
                            matrix[2 * g][2 * h + s],
                            matrix[2 * g + 1][2 * h + 1 - s],
                        )
                    )
                    for s in range(2)
                ]
                for h in range(2)
            ]
            for g in range(2)
        ]

    def quad_rows(matrix, segment):
        channel = (lane // segment) % 4
        rows = []
        for k in range(4):
            vector = jnp.zeros((1, LANES), F32)
            for i in range(4):
                vector = jnp.where(channel == i, matrix[i][(i - k) % 4], vector)
            rows.append(keep(vector))
        return rows

    S0, B0 = smooth_matrix(0), mix_matrix(0)
    T0 = product(S0, B0)
    smooth1, mixer1 = smooth_matrix(1), mix_matrix(1)
    S1, B1, T1 = pair_rows(smooth1), pair_rows(mixer1), pair_rows(product(smooth1, mixer1))
    smooth2, mixer2 = smooth_matrix(2), mix_matrix(2)
    S2, B2 = quad_rows(smooth2, 32), quad_rows(mixer2, 32)
    T2 = quad_rows(product(smooth2, mixer2), 32)
    smooth3, mixer3 = smooth_matrix(3), mix_matrix(3)
    S3, T3 = quad_rows(smooth3, 16), quad_rows(product(smooth3, mixer3), 16)

    def mixed4(matrix, fields):
        return [
            matrix[i][0] * fields[0]
            + matrix[i][1] * fields[1]
            + (matrix[i][2] * fields[2] + matrix[i][3] * fields[3])
            for i in range(4)
        ]

    def vector_of(row):
        return table[row : row + 1, :]

    def mixed2(rows, fields):
        turned = [pltpu.roll(field, 64, field.ndim - 1) for field in fields]
        return [
            vector_of(rows[g][0][0]) * fields[0]
            + vector_of(rows[g][0][1]) * turned[0]
            + (vector_of(rows[g][1][0]) * fields[1] + vector_of(rows[g][1][1]) * turned[1])
            for g in range(2)
        ]

    def mixed1(rows, field, segment):
        total = vector_of(rows[0]) * field
        for k in range(1, 4):
            total += vector_of(rows[k]) * pltpu.roll(field, k * segment, field.ndim - 1)
        return total

    wide, narrow = (2 * LANES, LANES), (LANES, LANES)

    def row_index(shape):
        return lax.broadcasted_iota(jnp.int32, shape, 0)

    down[...] = jnp.where(row_index(wide) // 2 == lane_index(wide), 0.125, 0.0).astype(BF16)
    up[...] = jnp.where(
        lane_index((LANES, 2 * LANES)) // 2 == row_index((LANES, 2 * LANES)), 1.0, 0.0
    ).astype(BF16)
    last_down[...] = jnp.where(
        row_index(narrow) // 2 == lane_index(narrow) % 64, 0.125, 0.0
    ).astype(BF16)
    last_up[...] = jnp.where(lane_index(narrow) // 2 == row_index(narrow), 1.0, 0.0).astype(BF16)

    started = []

    def send(src, dst, place):
        number = len(started)
        copy = pltpu.make_async_remote_copy(
            src_ref=src, dst_ref=dst, send_sem=send_sem.at[number], recv_sem=recv_sem.at[number],
            device_id=device(*place), device_id_type=MESH,
        )
        copy.start()
        started.append(copy)
        return copy

    def pack(g, s, planes, h, xs, ys):
        for p, (k, c) in enumerate(planes):
            s[0, p, 0:xs, :] = g[c, h : h + xs, PAD + k, :]
            s[1, p, 0:xs, :] = g[c, h : h + xs, PAD + ys - 1 - k, :]

    def exchange(g, s, p, corner, h, xs, ys, near):
        own = pl.ds(PAD, ys)
        copies = [
            send(g.at[:, pl.ds(xs, h), own], g.at[:, pl.ds(0, h), own], (1, 0)),
            send(g.at[:, pl.ds(h, h), own], g.at[:, pl.ds(xs + h, h), own], (-1, 0)),
            send(s.at[1], p.at[0], (0, 1)),
            send(s.at[0], p.at[1], (0, -1)),
        ]
        first, last = pl.ds(0, 8), pl.ds(max(xs - 8, 0), 8)
        for side, dy in ((1, 1), (0, -1)):
            for end, dx in ((last, 1), (first, -1)):
                copies.append(
                    send(
                        s.at[side, pl.ds(0, near), end],
                        corner.at[(0 if dx > 0 else 1) * 2 + (0 if dy > 0 else 1)],
                        (dx, dy),
                    )
                )
        return copies

    def unpack(copies, g, p, corner, planes, h, xs, ys, near, reach, a_reach):
        for copy in copies:
            copy.wait_recv()
        groups = g.shape[0]
        for n, (k, c) in enumerate(planes):
            g[c, h : h + xs, PAD - 1 - k, :] = p[0, n, 0:xs, :]
            g[c, h : h + xs, PAD + ys + k, :] = p[1, n, 0:xs, :]
        top = min(xs, 8) - 1
        for n, (k, c) in enumerate(planes[:near]):
            for i in range((a_reach if c == groups - 1 else reach) - 1 - k):
                for from_dy in range(2):
                    row = PAD - 1 - k if from_dy == 0 else PAD + ys + k
                    g[c, h - 1 - i, row : row + 1, :] = corner[from_dy, n, top - i : top - i + 1, :]
                    g[c, h + xs + i, row : row + 1, :] = corner[2 + from_dy, n, i : i + 1, :]

        @pl.when(mx == 0)
        def _():
            g[:, 0:h] = jnp.zeros((groups, h) + g.shape[2:], F32)

        @pl.when(mx == nx - 1)
        def _():
            g[:, h + xs :] = jnp.zeros((groups, h) + g.shape[2:], F32)

        @pl.when(my == 0)
        def _():
            g[:, :, 0:PAD] = jnp.zeros(g.shape[:2] + (PAD, LANES), F32)

        @pl.when(my == ny - 1)
        def _():
            g[:, :, PAD + ys :] = jnp.zeros(g.shape[:2] + (PAD, LANES), F32)

    def steps(count, body):
        def step(i, carry):
            body(i)
            return carry

        lax.fori_loop(0, count, step, 0)

    def stencil_of(field, coefficient, c, x, row, rows, segment):
        center = field[c, x, row : row + rows, :]
        beside = field[c, x - 1, row : row + rows, :] + field[c, x + 1, row : row + rows, :]
        beside += field[c, x, row - 1 : row - 1 + rows, :]
        beside += field[c, x, row + 1 : row + 1 + rows, :]
        return stencil(center, beside, coefficient, segment)

    for load in loads:
        load.wait()

    def smooth_fine(x):
        fields = mixed4(S0, [f0[c, x] for c in range(4)])
        for c in range(4):
            g0[c, x + 2, PAD : PAD + y0, :] = fields[c]

    steps(x0, smooth_fine)
    planes0 = [(0, 0), (0, 1), (0, 2), (0, 3), (0, 4), (1, 0), (1, 1), (1, 2), (1, 3)]
    pack(g0, s0, planes0, 2, x0, y0)
    pl.semaphore_wait(barrier, len(peers))
    copies = exchange(g0, s0, p0, c0, 2, x0, y0, 4)

    g1[2, 3 : 3 + x1, PAD : PAD + y1, :] = jnp.concatenate([a1[...]] * 2, axis=-1)
    g2[1, 3 : 3 + x2, PAD : PAD + y2, :] = jnp.concatenate([a2[...]] * 4, axis=-1)
    g3[1, 4 : 4 + x3, PAD : PAD + y3, :] = jnp.concatenate([a3[...]] * 8, axis=-1)
    unpack(copies, g0, p0, c0, planes0, 2, x0, y0, 4, 2, 1)

    def relax_fine(step):
        x = step + 1
        row, rows = PAD - 1, y0 + 2
        coefficient = g0[4, x, row : row + rows, :]
        change = mixed4(T0, [stencil_of(g0, coefficient, c, x, row, rows, LANES) for c in range(4)])
        for c in range(4):
            v0[c, x, row : row + rows, :] = 2.0 * g0[c, x, row : row + rows, :] - change[c]

    steps(x0 + 2, relax_fine)

    def residual_fine(i):
        total = [None] * 4
        for s in range(2):
            x = 2 * i + s
            coefficient = g0[4, x + 2, PAD : PAD + y0, :]
            applied = mixed4(
                B0, [stencil_of(v0, coefficient, c, x + 2, PAD, y0, LANES) for c in range(4)]
            )
            for c in range(4):
                rest = f0[c, x] - applied[c]
                total[c] = rest if s == 0 else total[c] + rest
        for c in range(4):
            r0[c, i] = total[c]

    steps(x1, residual_fine)

    for g in range(2):
        pieces = [
            r0[c, :, pl.ds(0, y1, stride=2), :] + r0[c, :, pl.ds(1, y1, stride=2), :]
            for c in (2 * g, 2 * g + 1)
        ]
        joined = jnp.concatenate([piece.reshape(x1 * y1, LANES) for piece in pieces], axis=-1)
        f1[g] = spread(joined, down[...]).reshape(x1, y1, LANES)
    fields = mixed2(S1, [f1[g] for g in range(2)])
    for g in range(2):
        g1[g, 3 : 3 + x1, PAD : PAD + y1, :] = fields[g]
    planes1 = [(0, 0), (0, 1), (0, 2), (1, 0), (1, 1), (1, 2), (2, 0), (2, 1)]
    pack(g1, s1, planes1, 3, x1, y1)
    copies = exchange(g1, s1, p1, c1, 3, x1, y1, 5)
    unpack(copies, g1, p1, c1, planes1, 3, x1, y1, 5, 3, 2)

    def relax_second(step):
        x = step + 1
        row, rows = PAD - 2, y1 + 4
        coefficient = g1[2, x, row : row + rows, :]
        change = mixed2(T1, [stencil_of(g1, coefficient, c, x, row, rows, 64) for c in range(2)])
        for c in range(2):
            v1[c, x, row : row + rows, :] = 2.0 * g1[c, x, row : row + rows, :] - change[c]

    steps(x1 + 4, relax_second)

    def residual_second(i):
        total = [None] * 2
        for s in range(2):
            x = 2 * i + s
            coefficient = g1[2, x + 3, PAD : PAD + y1, :]
            applied = mixed2(
                B1, [stencil_of(v1, coefficient, c, x + 3, PAD, y1, 64) for c in range(2)]
            )
            for c in range(2):
                rest = f1[c, x] - applied[c]
                total[c] = rest if s == 0 else total[c] + rest
        for c in range(2):
            r1[c, i] = total[c]

    steps(x2, residual_second)

    pieces = [
        r1[c, :, pl.ds(0, y2, stride=2), :] + r1[c, :, pl.ds(1, y2, stride=2), :] for c in range(2)
    ]
    joined = jnp.concatenate([piece.reshape(x2 * y2, LANES) for piece in pieces], axis=-1)
    f2[...] = spread(joined, down[...]).reshape(x2, y2, LANES)
    g2[0, 3 : 3 + x2, PAD : PAD + y2, :] = mixed1(S2, f2[...], 32)
    planes2 = [(0, 0), (0, 1), (1, 0), (1, 1), (2, 0)]
    pack(g2, s2, planes2, 3, x2, y2)
    copies = exchange(g2, s2, p2, c2, 3, x2, y2, 5)
    unpack(copies, g2, p2, c2, planes2, 3, x2, y2, 5, 4, 3)

    def block_stencil(load, coefficient, x, xs, row, rows, segment):
        center = load(x, xs, row, rows)
        beside = load(x - 1, xs, row, rows) + load(x + 1, xs, row, rows)
        beside += load(x, xs, row - 1, rows) + load(x, xs, row + 1, rows)
        return center, stencil(center, beside, coefficient, segment)

    def from_g2(x, xs, row, rows):
        return g2[0, x : x + xs, row : row + rows, :]

    def from_v2(x, xs, row, rows):
        return v2[x : x + xs, row : row + rows, :]

    row, rows = PAD - 2, y2 + 4
    center, applied = block_stencil(
        from_g2, g2[1, 1 : x2 + 5, row : row + rows, :], 1, x2 + 4, row, rows, 32
    )
    v2[1 : x2 + 5, row : row + rows, :] = 2.0 * center - mixed1(T2, applied, 32)
    _, applied = block_stencil(
        from_v2, g2[1, 3 : 3 + x2, PAD : PAD + y2, :], 3, x2, PAD, y2, 32
    )
    rest = f2[...] - mixed1(B2, applied, 32)
    pairs = jnp.concatenate([rest[2 * i] + rest[2 * i + 1] for i in range(x3)], axis=0)
    r3[...] = spread(pairs, last_down[...]).reshape(x3, y2, LANES)

    forcing = r3[:, pl.ds(0, y3, stride=2), :] + r3[:, pl.ds(1, y3, stride=2), :]
    smoothed = mixed1(S3, forcing, 16)
    g3[0, 4 : 4 + x3, PAD : PAD + y3, :] = smoothed
    s3[:, 0:y3, :] = smoothed
    s3[:, y3 : 2 * y3, :] = g3[1, 4 : 4 + x3, PAD : PAD + y3, :]
    for x in range(x3):
        line[x : x + 1, :] = jnp.sum(smoothed[x], axis=0, keepdims=True)
    copies = [send(s3, p3.at[0], (0, 1)), send(s3, p3.at[1], (0, -1))]
    copies += [send(line, lines.at[k - 1], (0, k)) for k in range(1, ny)]
    for copy in copies:
        copy.wait_recv()
    total = line[...]
    for k in range(1, ny):
        total += lines[k - 1]
    total *= 4.0 / math.sqrt(ny * y3)
    for x in range(x3):
        g3[0, 4 + x, 0:1, :] = total[x : x + 1, :]
    for side, row in ((0, PAD - y3), (1, PAD + y3)):
        inside = (my > 0) if side == 0 else (my < ny - 1)
        for c in range(2):
            g3[c, 4 : 4 + x3, row : row + y3, :] = jnp.where(
                inside, p3[side, :, c * y3 : (c + 1) * y3, :], 0.0
            )
    block = pl.ds(4, x3)
    used = pl.ds(0, 2 * PAD)
    copies = [
        send(g3.at[:, block, used], g3.at[:, pl.ds(4 - dx * x3, x3), used], (dx, 0))
        for dx in (1, -1, 2, -2)
    ]
    for copy in copies:
        copy.wait_recv()
    for dx in (1, -1, 2, -2):
        outside = (mx < dx) if dx > 0 else (mx >= nx + dx)

        @pl.when(outside)
        def _(dx=dx):
            g3[:, 4 - dx * x3 : 4 - dx * x3 + x3] = jnp.zeros((2, x3) + g3.shape[2:], F32)

    low, high = PAD - y3, PAD + 2 * y3
    cell = lax.broadcasted_iota(jnp.int32, (1, 3 * y3, LANES), 1) + (my - 1) * y3
    inside = (cell >= 0) & (cell < ny * y3)
    w3[:, low:high, :] = g3[0, :, low:high, :] + jnp.where(inside, g3[0, :, 0:1, :], 0.0)

    def from_w3(x, xs, row, rows):
        return w3[x : x + xs, row : row + rows, :]

    for sweep in range(1, 4):
        x, xs = sweep, 8 + x3 - 2 * sweep
        row, rows = low + sweep, high - low - 2 * sweep
        center, applied = block_stencil(
            from_w3, g3[1, x : x + xs, row : row + rows, :], x, xs, row, rows, 16
        )
        value = center + g3[0, x : x + xs, row : row + rows, :] - mixed1(T3, applied, 16)
        if sweep < 3:
            w3[x : x + xs, row : row + rows, :] = value
        else:
            b3[:, 0:rows, :] = value

    xs, rows = x3 + 2, y3 + 2
    children = spread(b3[...].reshape(xs * 8, LANES), last_up[...]).reshape(xs, 8, LANES)
    for i in range(xs):
        for s in range(2):
            q2[i, pl.ds(PAD - 2 + s, rows, stride=2), :] = children[i, 0:rows, :]
    row, rows = PAD - 2, y2 + 4
    for i in range(xs):
        for s in range(2):
            v2[1 + 2 * i + s, row : row + rows, :] += q2[i, row : row + rows, :]
    row, rows = PAD - 1, y2 + 2
    center, applied = block_stencil(
        from_v2, g2[1, 2 : x2 + 4, row : row + rows, :], 2, x2 + 2, row, rows, 32
    )
    w2[:, 0:rows, :] = center + g2[0, 2 : x2 + 4, row : row + rows, :] - mixed1(T2, applied, 32)

    xs = x2 + 2
    children = spread(w2[...].reshape(xs * 16, LANES), up[...]).reshape(xs, 16, 2 * LANES)
    for g in range(2):
        for i in range(xs):
            for s in range(2):
                q1[g, i, pl.ds(PAD - 2 + s, rows, stride=2), :] = children[
                    i, 0:rows, g * LANES : (g + 1) * LANES
                ]

    def lift_second(step):
        row, rows = PAD - 2, y1 + 4
        for g in range(2):
            part = q1[g, step // 2, row : row + rows, :]
            v1[g, step + 1, row : row + rows, :] += part

    steps(x1 + 4, lift_second)

    def finish_second(step):
        x = step + 2
        row, rows = PAD - 1, y1 + 2
        coefficient = g1[2, x, row : row + rows, :]
        change = mixed2(T1, [stencil_of(v1, coefficient, c, x, row, rows, 64) for c in range(2)])
        for c in range(2):
            value = v1[c, x, row : row + rows, :] + g1[c, x, row : row + rows, :] - change[c]
            w1[c, step, 0:rows, :] = value

    steps(x1 + 2, finish_second)

    def spread_fine(i):
        rows = y1 + 2
        for g in range(2):
            children = spread(w1[g, i], up[...])
            for c in range(2):
                for s in range(2):
                    q0[2 * g + c, i, pl.ds(PAD - 2 + s, rows, stride=2), :] = children[
                        0:rows, c * LANES : (c + 1) * LANES
                    ]

    steps(x1 + 2, spread_fine)

    def lift_fine(step):
        row, rows = PAD - 1, y0 + 2
        for c in range(4):
            part = q0[c, (step + 1) // 2, row : row + rows, :]
            v0[c, step + 1, row : row + rows, :] += part

    steps(x0 + 2, lift_fine)

    def finish_fine(x):
        coefficient = g0[4, x + 2, PAD : PAD + y0, :]
        change = mixed4(
            T0, [stencil_of(v0, coefficient, c, x + 2, PAD, y0, LANES) for c in range(4)]
        )
        for c in range(4):
            value = v0[c, x + 2, PAD : PAD + y0, :] + g0[c, x + 2, PAD : PAD + y0, :]
            f0[c, x] = value - change[c]

    quarter = x0 // 4
    stores = []
    for q in range(4):
        steps(quarter, lambda i, q=q: finish_fine(i + q * quarter))
        part = pl.ds(q * quarter, quarter)
        store = pltpu.make_async_copy(f0.at[:, part], out.at[:, part], out_sem.at[q])
        store.start()
        stores.append(store)
    for copy in started:
        copy.wait_send()
    for store in stores:
        store.wait()


def per_device(nx, ny, source, fine, second, third, coarse, mixers, smoothers):
    x0, y0 = source.shape[1:3]
    x1, y1 = second.shape[:2]
    x2, y2 = third.shape[:2]
    x3, y3 = coarse.shape[:2]

    def padded(groups, xs, ys, h):
        return pltpu.VMEM((groups, xs + 2 * h, ys + 2 * PAD, LANES), F32)

    def vmem(*shape):
        return pltpu.VMEM(shape, F32)

    def faces(planes, near, xs):
        rows = max(xs, 8)
        return [
            vmem(2, planes, rows, LANES),
            vmem(2, planes, rows, LANES),
            vmem(4, near, 8, LANES),
        ]

    scratch = (
        [vmem(4, x0, y0, LANES), padded(5, x0, y0, 2), padded(4, x0, y0, 2)]
        + [vmem(4, x1, y0, LANES), vmem(4, x1 + 2, y0 + 2 * PAD, LANES)]
        + faces(9, 4, x0)
        + [vmem(*second.shape), vmem(2, x1, y1, LANES), padded(3, x1, y1, 3), padded(2, x1, y1, 3)]
        + [vmem(2, x2, y1, LANES), vmem(2, x2 + 2, y1 + 2 * PAD, LANES)]
        + [vmem(2, x1 + 2, y1 + 8, LANES)]
        + faces(8, 5, x1)
        + [vmem(*third.shape), vmem(x2, y2, LANES), padded(2, x2, y2, 3)]
        + [vmem(x2 + 6, y2 + 2 * PAD, LANES), vmem(x3, y2, LANES)]
        + [vmem(x3 + 2, y2 + 2 * PAD, LANES), vmem(x2 + 2, 16, LANES)]
        + faces(5, 5, x2)
        + [vmem(*coarse.shape), vmem(x3, y2, LANES), vmem(2, x3 + 8, 24, LANES)]
        + [vmem(x3 + 8, 24, LANES), vmem(x3 + 2, 8, LANES)]
        + [vmem(x3, 2 * y3, LANES), vmem(2, x3, 2 * y3, LANES)]
        + [vmem(x3, LANES), vmem(ny - 1, x3, LANES)]
        + [vmem(48, LANES)]
        + [pltpu.VMEM((2 * LANES, LANES), BF16), pltpu.VMEM((LANES, 2 * LANES), BF16)]
        + [pltpu.VMEM((LANES, LANES), BF16), pltpu.VMEM((LANES, LANES), BF16)]
    )
    copies = 8 * 3 + 2 + (ny - 1) + 4
    scratch += [
        pltpu.SemaphoreType.DMA((copies,)),
        pltpu.SemaphoreType.DMA((copies,)),
        pltpu.SemaphoreType.DMA((5,)),
        pltpu.SemaphoreType.DMA((4,)),
    ]
    anywhere = pl.BlockSpec(memory_space=pl.ANY)
    scalars = pl.BlockSpec(memory_space=pltpu.SMEM)
    return pl.pallas_call(
        functools.partial(kernel, nx, ny),
        out_shape=jax.ShapeDtypeStruct(source.shape, F32),
        in_specs=[anywhere] * 5 + [scalars] * 2,
        out_specs=anywhere,
        scratch_shapes=scratch,
        compiler_params=pltpu.CompilerParams(
            collective_id=0, has_side_effects=True, vmem_limit_bytes=40 * 1024 * 1024
        ),
    )(source, fine, second, third, coarse, mixers, smoothers)


def solution(mesh):
    field, cells = P(None, "gx", "gy", None), P("gx", "gy", None)
    return jax.shard_map(
        functools.partial(per_device, mesh.shape["gx"], mesh.shape["gy"]),
        mesh=mesh,
        in_specs=(field, cells, cells, cells, cells, P(), P()),
        out_specs=field,
        check_vma=False,
    )
```

profile of v0, /device:TPU:1, one launch (start us, length us, event | category | flops | bytes accessed | tf_op | source)
XLA Modules:
  0.0 71.5 jit_solution(4878485353549670992)
XLA Ops:
  0.0 0.0 copy-start
  0.0 1.2 %copy-done = f32[4,16,32,128]{3,2,1,0:T(8,128)S(1)} copy-done((f32[4,16,32,128]{3,2,1,0:T(8,128)S(1)}, f32[4,16,32,128]{3,2,1,0:T(8,128)}, u32[]{:S(2)}) %copy-start) | copy-done | bytes 1048600
  1.2 0.0 copy-start.1
  1.2 0.9 %copy-done.1 = f32[16,32,128]{2,1,0:T(8,128)S(1)} copy-done((f32[16,32,128]{2,1,0:T(8,128)S(1)}, f32[16,32,128]{2,1,0:T(8,128)}, u32[]{:S(2)}) %copy-start.1) | copy-done | bytes 262168
  2.2 0.0 copy-start.2
  2.2 0.8 %copy-done.2 = f32[8,16,64]{2,1,0:T(8,128)S(1)} copy-done((f32[8,16,64]{2,1,0:T(8,128)S(1)}, f32[8,16,64]{2,1,0:T(8,128)}, u32[]{:S(2)}) %copy-start.2) | copy-done | bytes 32792
  3.0 0.0 copy-start.3
  3.0 0.7 %copy-done.3 = f32[4,8,32]{2,1,0:T(8,128)S(1)} copy-done((f32[4,8,32]{2,1,0:T(8,128)S(1)}, f32[4,8,32]{2,1,0:T(8,128)}, u32[]{:S(2)}) %copy-start.3) | copy-done | bytes 4120
  3.7 0.0 copy-start.4
  3.7 0.7 copy-done.4
  4.4 0.0 copy-start.5
  4.4 0.7 copy-done.5
  5.1 0.0 copy-start.6
  5.1 0.7 copy-done.6
  5.8 64.7 %shard_map.73 = f32[4,16,32,128]{3,2,1,0:T(8,128)S(1)} custom-call(f32[4,16,32,128]{3,2,1,0:T(8,128)S(1)} %copy-done, f32[16,32,128]{2,1,0:T(8,128)S(1)} %copy-done.1, f32[8,16,64]{2,1,0:T(8,128)S(1)} %copy-done.2, f32[4,8,32]{2,1,0:T(8,128)S(1)} %copy-done.3, f32[2,4,16]{2,1,0:T(4,128)S(1)} %copy-done.6, f32[4,4,4]{2,1,0:T(4,128)S(1)} %copy-done.4, ...), custom_call_target="tpu_custom_call" | custom-call | tf_op jit(solution)/shard_map/pallas_call | solution.py:577
  70.5 1.0 %copy.9 = f32[4,16,32,128]{3,2,1,0:T(8,128)} copy(f32[4,16,32,128]{3,2,1,0:T(8,128)S(1)} %shard_map.73) | data formatting | bytes 2097152
Async XLA Ops:
  0.0 1.2 %copy-start = (f32[4,16,32,128]{3,2,1,0:T(8,128)S(1)}, f32[4,16,32,128]{3,2,1,0:T(8,128)}, u32[]{:S(2)}) copy-start(f32[4,16,32,128]{3,2,1,0:T(8,128)} %source.1) | copy-start | bytes 3145732
  1.2 0.9 %copy-start.1 = (f32[16,32,128]{2,1,0:T(8,128)S(1)}, f32[16,32,128]{2,1,0:T(8,128)}, u32[]{:S(2)}) copy-start(f32[16,32,128]{2,1,0:T(8,128)} %fine.1) | copy-start | bytes 786436
  2.2 0.8 %copy-start.2 = (f32[8,16,64]{2,1,0:T(8,128)S(1)}, f32[8,16,64]{2,1,0:T(8,128)}, u32[]{:S(2)}) copy-start(f32[8,16,64]{2,1,0:T(8,128)} %second.1) | copy-start | bytes 98308
  3.0 0.7 %copy-start.3 = (f32[4,8,32]{2,1,0:T(8,128)S(1)}, f32[4,8,32]{2,1,0:T(8,128)}, u32[]{:S(2)}) copy-start(f32[4,8,32]{2,1,0:T(8,128)} %third.1) | copy-start | bytes 12292
  3.7 0.7 copy-start.4
  4.4 0.7 copy-start.5
  5.1 0.7 copy-start.6
where the time goes:
time: 71.9 us; the launch traced here: 71.5 us
  Pallas kernels  64.7 us (90%)
  local copies, waits for them, and re-layouts  6.78 us (9%)
    pallas_call x1, Pallas kernels, per_device(): pl.pallas_call(functools.partial(kernel, nx, ny), out_shape=jax.ShapeDtyp...  64.7 us
    unnamed x15, local copies, waits for them, and re-layouts  6.78 us

commit v1 on v0

--- a/solution.py
+++ b/solution.py
@@ -23,6 +23,12 @@
     )
 
 
+def spread_stacked(field, matrix):
+    high = field.astype(BF16)
+    low = (field - high.astype(F32)).astype(BF16)
+    return jnp.dot(jnp.concatenate([high, low], axis=-1), matrix, preferred_element_type=F32)
+
+
 def lane_index(shape):
     return lax.broadcasted_iota(jnp.int32, shape, len(shape) - 1)
 
@@ -43,11 +49,11 @@
 def kernel(
     nx, ny,
     source, fine, second, third, coarse, mixers, smoothers, out,
-    f0, g0, v0, r0, q0, s0, p0, c0,
-    a1, f1, g1, v1, r1, q1, w1, s1, p1, c1,
-    a2, f2, g2, v2, r2, q2, w2, s2, p2, c2,
-    a3, r3, g3, w3, b3, s3, p3, line, lines,
-    table, down, up, last_down, last_up,
+    f0, a0, g0, v0, h0, r0, e0, m0, q0, s0, p0, c0,
+    a1, f1, g1, v1, r1, x1_part, e1, m1, q1, w1, s1, p1, c1,
+    a2, f2, g2, v2, r2, x2_part, e2, m2, q2, w2, s2, p2, c2,
+    a3, r3, g3, k3, w3, b3, s3, p3, t3, u3, line, lines,
+    table, down, up, rise_fine, rise_second, last_down, last_up, last_rise,
     send_sem, recv_sem, local_sem, out_sem,
 ):
     mx, my = lax.axis_index("gx"), lax.axis_index("gy")
@@ -65,14 +71,21 @@
     x1, y1 = f1.shape[1:3]
     x2, y2 = f2.shape[:2]
     x3, y3 = a3.shape[:2]
-    loads = [
-        pltpu.make_async_copy(source, f0, local_sem.at[0]),
-        pltpu.make_async_copy(fine, g0.at[4, pl.ds(2, x0), pl.ds(PAD, y0)], local_sem.at[1]),
-        pltpu.make_async_copy(second, a1, local_sem.at[2]),
-        pltpu.make_async_copy(third, a2, local_sem.at[3]),
-        pltpu.make_async_copy(coarse, a3, local_sem.at[4]),
+    first_rows = min(4, x0 // 4)
+    parts = [(0, first_rows), (x0 - first_rows, first_rows), (first_rows, x0 - 2 * first_rows)]
+    load_fine = pltpu.make_async_copy(fine, a0.at[pl.ds(1, x0)], local_sem.at[0])
+    load_parts = [
+        pltpu.make_async_copy(
+            source.at[:, pl.ds(x, xs)], f0.at[:, pl.ds(x, xs)], local_sem.at[4 + n]
+        )
+        for n, (x, xs) in enumerate(parts)
     ]
-    for load in loads:
+    load_coarser = [
+        pltpu.make_async_copy(second, a1, local_sem.at[1]),
+        pltpu.make_async_copy(third, a2, local_sem.at[2]),
+        pltpu.make_async_copy(coarse, a3, local_sem.at[3]),
+    ]
+    for load in load_parts + [load_fine] + load_coarser:
         load.start()
 
     def smooth_matrix(level):
@@ -128,15 +141,7 @@
             rows.append(keep(vector))
         return rows
 
-    S0, B0 = smooth_matrix(0), mix_matrix(0)
-    T0 = product(S0, B0)
-    smooth1, mixer1 = smooth_matrix(1), mix_matrix(1)
-    S1, B1, T1 = pair_rows(smooth1), pair_rows(mixer1), pair_rows(product(smooth1, mixer1))
-    smooth2, mixer2 = smooth_matrix(2), mix_matrix(2)
-    S2, B2 = quad_rows(smooth2, 32), quad_rows(mixer2, 32)
-    T2 = quad_rows(product(smooth2, mixer2), 32)
-    smooth3, mixer3 = smooth_matrix(3), mix_matrix(3)
-    S3, T3 = quad_rows(smooth3, 16), quad_rows(product(smooth3, mixer3), 16)
+    S0 = smooth_matrix(0)
 
     def mixed4(matrix, fields):
         return [
@@ -164,19 +169,20 @@
             total += vector_of(rows[k]) * pltpu.roll(field, k * segment, field.ndim - 1)
         return total
 
-    wide, narrow = (2 * LANES, LANES), (LANES, LANES)
-
     def row_index(shape):
         return lax.broadcasted_iota(jnp.int32, shape, 0)
 
-    down[...] = jnp.where(row_index(wide) // 2 == lane_index(wide), 0.125, 0.0).astype(BF16)
-    up[...] = jnp.where(
-        lane_index((LANES, 2 * LANES)) // 2 == row_index((LANES, 2 * LANES)), 1.0, 0.0
-    ).astype(BF16)
-    last_down[...] = jnp.where(
-        row_index(narrow) // 2 == lane_index(narrow) % 64, 0.125, 0.0
-    ).astype(BF16)
-    last_up[...] = jnp.where(lane_index(narrow) // 2 == row_index(narrow), 1.0, 0.0).astype(BF16)
+    def children_matrix(columns, segment):
+        shape = (2 * LANES, columns)
+        row, column = row_index(shape) % LANES, lane_index(shape)
+        if segment is None:
+            return jnp.where(row == column // 2, 1.0, 0.0).astype(BF16)
+        odd = column % 2
+        other = column // 2 + 2 * odd - 1
+        place = column % segment
+        valid = (place != 0) & (place != segment - 1)
+        own = jnp.where(row == column // 2, 3.0, 0.0)
+        return (own - jnp.where((row == other) & valid, 1.0, 0.0)).astype(BF16)
 
     started = []
 
@@ -195,14 +201,8 @@
             s[0, p, 0:xs, :] = g[c, h : h + xs, PAD + k, :]
             s[1, p, 0:xs, :] = g[c, h : h + xs, PAD + ys - 1 - k, :]
 
-    def exchange(g, s, p, corner, h, xs, ys, near):
-        own = pl.ds(PAD, ys)
-        copies = [
-            send(g.at[:, pl.ds(xs, h), own], g.at[:, pl.ds(0, h), own], (1, 0)),
-            send(g.at[:, pl.ds(h, h), own], g.at[:, pl.ds(xs + h, h), own], (-1, 0)),
-            send(s.at[1], p.at[0], (0, 1)),
-            send(s.at[0], p.at[1], (0, -1)),
-        ]
+    def send_corners(s, corner, xs, near):
+        copies = []
         first, last = pl.ds(0, 8), pl.ds(max(xs - 8, 0), 8)
         for side, dy in ((1, 1), (0, -1)):
             for end, dx in ((last, 1), (first, -1)):
@@ -214,6 +214,16 @@
                     )
                 )
         return copies
+
+    def exchange(g, s, p, corner, h, xs, ys, near):
+        own = pl.ds(PAD, ys)
+        copies = [
+            send(g.at[:, pl.ds(xs, h), own], g.at[:, pl.ds(0, h), own], (1, 0)),
+            send(g.at[:, pl.ds(h, h), own], g.at[:, pl.ds(xs + h, h), own], (-1, 0)),
+            send(s.at[1], p.at[0], (0, 1)),
+            send(s.at[0], p.at[1], (0, -1)),
+        ]
+        return copies + send_corners(s, corner, xs, near)
 
     def unpack(copies, g, p, corner, planes, h, xs, ys, near, reach, a_reach):
         for copy in copies:
@@ -260,43 +270,157 @@
         beside += field[c, x, row + 1 : row + 1 + rows, :]
         return stencil(center, beside, coefficient, segment)
 
-    for load in loads:
-        load.wait()
+    y_rows = y0 + 2 * PAD
+
+    def fine_rows(buffer, c, x, row, rows):
+        start = x * y_rows + row
+        if row % 8 == 0:
+            start = pl.multiple_of(start, 8)
+        return buffer[c, pl.ds(start, rows), :]
+
+    def fine_plane(row):
+        return pl.ds(2 * y_rows + row, x0, stride=y_rows)
+
+    def fine_stencil(buffer, coefficient, c, x):
+        center = fine_rows(buffer, c, x, PAD, y0)
+        beside = fine_rows(buffer, c, x - 1, PAD, y0) + fine_rows(buffer, c, x + 1, PAD, y0)
+        beside += fine_rows(buffer, c, x, PAD - 1, y0) + fine_rows(buffer, c, x, PAD + 1, y0)
+        return stencil(center, beside, coefficient, LANES)
 
     def smooth_fine(x):
         fields = mixed4(S0, [f0[c, x] for c in range(4)])
         for c in range(4):
-            g0[c, x + 2, PAD : PAD + y0, :] = fields[c]
-
-    steps(x0, smooth_fine)
-    planes0 = [(0, 0), (0, 1), (0, 2), (0, 3), (0, 4), (1, 0), (1, 1), (1, 2), (1, 3)]
-    pack(g0, s0, planes0, 2, x0, y0)
+            start = pl.multiple_of((x + 2) * y_rows + PAD, 8)
+            g0[c, pl.ds(start, y0), :] = fields[c]
+
+    def smooth_part(n):
+        load_parts[n].wait()
+        x, xs = parts[n]
+        steps(xs, lambda i: smooth_fine(i + x))
+
+    smooth_part(0)
+    smooth_part(1)
+    load_fine.wait()
     pl.semaphore_wait(barrier, len(peers))
-    copies = exchange(g0, s0, p0, c0, 2, x0, y0, 4)
-
+    copies = []
+    for layer, dst, dx in ((x0 + 1, 1, 1), (2, x0 + 2, -1), (x0, 0, 1), (3, x0 + 3, -1)):
+        copies.append(
+            send(
+                g0.at[:, pl.ds(layer * y_rows + PAD, y0)],
+                g0.at[:, pl.ds(dst * y_rows + PAD, y0)],
+                (dx, 0),
+            )
+        )
+    copies.append(send(a0.at[pl.ds(x0, 1)], a0.at[pl.ds(0, 1)], (1, 0)))
+    copies.append(send(a0.at[pl.ds(1, 1)], a0.at[pl.ds(x0 + 1, 1)], (-1, 0)))
+    smooth_part(2)
+    for c in range(4):
+        for k in range(2):
+            n = c if k == 0 else 5 + c
+            s0[0, n] = g0[c, fine_plane(PAD + k), :]
+            s0[1, n] = g0[c, fine_plane(PAD + y0 - 1 - k), :]
+    s0[0, 4] = a0[1 : x0 + 1, 0, :]
+    s0[1, 4] = a0[1 : x0 + 1, y0 - 1, :]
+    copies.append(send(s0.at[1], p0.at[0], (0, 1)))
+    copies.append(send(s0.at[0], p0.at[1], (0, -1)))
+    copies += send_corners(s0, c0, x0, 4)
+
+    for c in range(4):
+        for row in (PAD - 1, PAD + y0):
+            g0[c, fine_plane(row), :] = jnp.zeros((x0, LANES), F32)
+    B0 = mix_matrix(0)
+    T0 = product(S0, B0)
+
+    def relax_fine(x):
+        coefficient = a0[x - 1]
+        change = mixed4(T0, [fine_stencil(g0, coefficient, c, x) for c in range(4)])
+        for c in range(4):
+            value = 2.0 * fine_rows(g0, c, x, PAD, y0) - change[c]
+            v0[c, pl.ds(pl.multiple_of(x * y_rows + PAD, 8), y0), :] = value
+
+    steps(x0 - 2, lambda i: relax_fine(i + 3))
+    for load in load_coarser:
+        load.wait()
+    third_cells = jnp.concatenate([a3[...]] * 8, axis=-1)
+    k3[4 : 4 + x3, PAD : PAD + y3, :] = third_cells
+    for x in range(x3):
+        t3[x * y3 : (x + 1) * y3, :] = third_cells[x]
+    coarse_copies = [send(t3, u3.at[0], (0, 1)), send(t3, u3.at[1], (0, -1))]
     g1[2, 3 : 3 + x1, PAD : PAD + y1, :] = jnp.concatenate([a1[...]] * 2, axis=-1)
     g2[1, 3 : 3 + x2, PAD : PAD + y2, :] = jnp.concatenate([a2[...]] * 4, axis=-1)
-    g3[1, 4 : 4 + x3, PAD : PAD + y3, :] = jnp.concatenate([a3[...]] * 8, axis=-1)
-    unpack(copies, g0, p0, c0, planes0, 2, x0, y0, 4, 2, 1)
-
-    def relax_fine(step):
-        x = step + 1
-        row, rows = PAD - 1, y0 + 2
-        coefficient = g0[4, x, row : row + rows, :]
-        change = mixed4(T0, [stencil_of(g0, coefficient, c, x, row, rows, LANES) for c in range(4)])
+    smooth1, mixer1 = smooth_matrix(1), mix_matrix(1)
+    S1, B1, T1 = pair_rows(smooth1), pair_rows(mixer1), pair_rows(product(smooth1, mixer1))
+    smooth2, mixer2 = smooth_matrix(2), mix_matrix(2)
+    S2, B2 = quad_rows(smooth2, 32), quad_rows(mixer2, 32)
+    T2 = quad_rows(product(smooth2, mixer2), 32)
+    smooth3, mixer3 = smooth_matrix(3), mix_matrix(3)
+    S3, T3 = quad_rows(smooth3, 16), quad_rows(product(smooth3, mixer3), 16)
+    T0_below = pair_rows(T0)
+    T1_below = quad_rows(product(smooth1, mixer1), 32)
+    T2_below = quad_rows(product(smooth2, mixer2), 16)
+
+    wide, narrow = (2 * LANES, LANES), (LANES, LANES)
+    down[...] = jnp.where(row_index(wide) // 2 == lane_index(wide), 0.125, 0.0).astype(BF16)
+    last_down[...] = jnp.where(
+        row_index(narrow) // 2 == lane_index(narrow) % 64, 0.125, 0.0
+    ).astype(BF16)
+    up[...] = children_matrix(2 * LANES, None)
+    rise_fine[...] = children_matrix(2 * LANES, LANES)
+    rise_second[...] = children_matrix(2 * LANES, 64)
+    last_up[...] = children_matrix(LANES, None)
+    last_rise[...] = children_matrix(LANES, 32)
+
+    for copy in copies:
+        copy.wait_recv()
+
+    @pl.when(mx == 0)
+    def _():
+        g0[:, 0 : 2 * y_rows] = jnp.zeros((4, 2 * y_rows, LANES), F32)
+        c0[0:2] = jnp.zeros((2,) + c0.shape[1:], F32)
+        a0[0] = jnp.zeros((y0, LANES), F32)
+
+    @pl.when(mx == nx - 1)
+    def _():
+        g0[:, (x0 + 2) * y_rows :] = jnp.zeros((4, 2 * y_rows, LANES), F32)
+        c0[2:4] = jnp.zeros((2,) + c0.shape[1:], F32)
+        a0[x0 + 1] = jnp.zeros((y0, LANES), F32)
+
+    for side, edge in ((0, 0), (1, ny - 1)):
+
+        @pl.when(my == edge)
+        def _(side=side):
+            p0[side] = jnp.zeros(p0.shape[1:], F32)
+            c0[side] = jnp.zeros(c0.shape[1:], F32)
+            c0[2 + side] = jnp.zeros(c0.shape[1:], F32)
+
+    for c in range(4):
+        for side, row in ((0, PAD - 1), (1, PAD + y0)):
+            left, right = c0[side, c, 7:8, :], c0[2 + side, c, 0:1, :]
+            g0[c, y_rows + row : y_rows + row + 1, :] = left
+            g0[c, (x0 + 2) * y_rows + row : (x0 + 2) * y_rows + row + 1, :] = right
+            h0[side, c, PAD - 1 : PAD, :] = left
+            h0[side, c, PAD + x0 : PAD + x0 + 1, :] = right
+            h0[side, c, PAD : PAD + x0, :] = p0[side, c]
+    steps(4, lambda i: relax_fine(1 + i + (x0 - 2) * (i // 2)))
+    for side, own, halo in ((0, PAD, PAD - 1), (1, PAD + y0 - 1, PAD + y0)):
+        near = [p0[side, c] for c in range(4)]
+        change = mixed4(T0, [s0[side, 4] * near[c] for c in range(4)])
         for c in range(4):
-            v0[c, x, row : row + rows, :] = 2.0 * g0[c, x, row : row + rows, :] - change[c]
-
-    steps(x0 + 2, relax_fine)
+            v0[c, fine_plane(own), :] += change[c]
+        applied = []
+        for c in range(4):
+            beside = h0[side, c, PAD - 1 : PAD - 1 + x0, :] + h0[side, c, PAD + 1 : PAD + 1 + x0, :]
+            beside += p0[side, 5 + c] + s0[side, c]
+            applied.append(stencil(near[c], beside, p0[side, 4], LANES))
+        change = mixed4(T0, applied)
+        for c in range(4):
+            v0[c, fine_plane(halo), :] = 2.0 * near[c] - change[c]
 
     def residual_fine(i):
         total = [None] * 4
         for s in range(2):
             x = 2 * i + s
-            coefficient = g0[4, x + 2, PAD : PAD + y0, :]
-            applied = mixed4(
-                B0, [stencil_of(v0, coefficient, c, x + 2, PAD, y0, LANES) for c in range(4)]
-            )
+            applied = mixed4(B0, [fine_stencil(v0, a0[x + 1], c, x + 2) for c in range(4)])
             for c in range(4):
                 rest = f0[c, x] - applied[c]
                 total[c] = rest if s == 0 else total[c] + rest
@@ -318,6 +442,44 @@
     planes1 = [(0, 0), (0, 1), (0, 2), (1, 0), (1, 1), (1, 2), (2, 0), (2, 1)]
     pack(g1, s1, planes1, 3, x1, y1)
     copies = exchange(g1, s1, p1, c1, 3, x1, y1, 5)
+
+    def fill_beside(buffer, received):
+        for side, row in ((0, PAD - y3), (1, PAD + y3)):
+            inside = (my > 0) if side == 0 else (my < ny - 1)
+            for x in range(x3):
+                buffer[4 + x, row : row + y3, :] = jnp.where(
+                    inside, received[side, x * y3 : (x + 1) * y3, :], 0.0
+                )
+
+    def send_block(buffer):
+        block, used = pl.ds(4, x3), pl.ds(0, 2 * PAD)
+        return [
+            send(buffer.at[block, used], buffer.at[pl.ds(4 - dx * x3, x3), used], (dx, 0))
+            for dx in (1, -1, 2, -2)
+        ]
+
+    def receive_block(buffer, copies):
+        for copy in copies:
+            copy.wait_recv()
+        for dx in (1, -1, 2, -2):
+            outside = (mx < dx) if dx > 0 else (mx >= nx + dx)
+
+            @pl.when(outside)
+            def _(dx=dx):
+                buffer[4 - dx * x3 : 4 - dx * x3 + x3] = jnp.zeros((x3,) + buffer.shape[1:], F32)
+
+    for copy in coarse_copies:
+        copy.wait_recv()
+    fill_beside(k3, u3)
+    coarse_copies = send_block(k3)
+
+    def settle_fine(x):
+        change = mixed4(T0, [fine_stencil(v0, a0[x + 1], c, x + 2) for c in range(4)])
+        for c in range(4):
+            value = fine_rows(v0, c, x + 2, PAD, y0) + fine_rows(g0, c, x + 2, PAD, y0)
+            f0[c, x] = value - change[c]
+
+    steps(x0, settle_fine)
     unpack(copies, g1, p1, c1, planes1, 3, x1, y1, 5, 3, 2)
 
     def relax_second(step):
@@ -355,6 +517,18 @@
     planes2 = [(0, 0), (0, 1), (1, 0), (1, 1), (2, 0)]
     pack(g2, s2, planes2, 3, x2, y2)
     copies = exchange(g2, s2, p2, c2, 3, x2, y2, 5)
+    receive_block(k3, coarse_copies)
+
+    def settle_second(step):
+        x = step + 2
+        row, rows = PAD - 1, y1 + 2
+        coefficient = g1[2, x, row : row + rows, :]
+        change = mixed2(T1, [stencil_of(v1, coefficient, c, x, row, rows, 64) for c in range(2)])
+        for c in range(2):
+            value = v1[c, x, row : row + rows, :] + g1[c, x, row : row + rows, :] - change[c]
+            x1_part[c, step, row : row + rows, :] = value
+
+    steps(x1 + 2, settle_second)
     unpack(copies, g2, p2, c2, planes2, 3, x2, y2, 5, 4, 3)
 
     def block_stencil(load, coefficient, x, xs, row, rows, segment):
@@ -383,13 +557,19 @@
 
     forcing = r3[:, pl.ds(0, y3, stride=2), :] + r3[:, pl.ds(1, y3, stride=2), :]
     smoothed = mixed1(S3, forcing, 16)
-    g3[0, 4 : 4 + x3, PAD : PAD + y3, :] = smoothed
-    s3[:, 0:y3, :] = smoothed
-    s3[:, y3 : 2 * y3, :] = g3[1, 4 : 4 + x3, PAD : PAD + y3, :]
+    g3[4 : 4 + x3, PAD : PAD + y3, :] = smoothed
     for x in range(x3):
+        s3[x * y3 : (x + 1) * y3, :] = smoothed[x]
         line[x : x + 1, :] = jnp.sum(smoothed[x], axis=0, keepdims=True)
-    copies = [send(s3, p3.at[0], (0, 1)), send(s3, p3.at[1], (0, -1))]
-    copies += [send(line, lines.at[k - 1], (0, k)) for k in range(1, ny)]
+    copies = [send(line, lines.at[k - 1], (0, k)) for k in range(1, ny)]
+    copies += [send(s3, p3.at[0], (0, 1)), send(s3, p3.at[1], (0, -1))]
+    row, rows = PAD - 1, y2 + 2
+    center, applied = block_stencil(
+        from_v2, g2[1, 2 : x2 + 4, row : row + rows, :], 2, x2 + 2, row, rows, 32
+    )
+    x2_part[:, row : row + rows, :] = (
+        center + g2[0, 2 : x2 + 4, row : row + rows, :] - mixed1(T2, applied, 32)
+    )
     for copy in copies:
         copy.wait_recv()
     total = line[...]
@@ -397,32 +577,14 @@
         total += lines[k - 1]
     total *= 4.0 / math.sqrt(ny * y3)
     for x in range(x3):
-        g3[0, 4 + x, 0:1, :] = total[x : x + 1, :]
-    for side, row in ((0, PAD - y3), (1, PAD + y3)):
-        inside = (my > 0) if side == 0 else (my < ny - 1)
-        for c in range(2):
-            g3[c, 4 : 4 + x3, row : row + y3, :] = jnp.where(
-                inside, p3[side, :, c * y3 : (c + 1) * y3, :], 0.0
-            )
-    block = pl.ds(4, x3)
-    used = pl.ds(0, 2 * PAD)
-    copies = [
-        send(g3.at[:, block, used], g3.at[:, pl.ds(4 - dx * x3, x3), used], (dx, 0))
-        for dx in (1, -1, 2, -2)
-    ]
-    for copy in copies:
-        copy.wait_recv()
-    for dx in (1, -1, 2, -2):
-        outside = (mx < dx) if dx > 0 else (mx >= nx + dx)
-
-        @pl.when(outside)
-        def _(dx=dx):
-            g3[:, 4 - dx * x3 : 4 - dx * x3 + x3] = jnp.zeros((2, x3) + g3.shape[2:], F32)
+        g3[4 + x, 0:1, :] = total[x : x + 1, :]
+    fill_beside(g3, p3)
+    receive_block(g3, send_block(g3))
 
     low, high = PAD - y3, PAD + 2 * y3
     cell = lax.broadcasted_iota(jnp.int32, (1, 3 * y3, LANES), 1) + (my - 1) * y3
     inside = (cell >= 0) & (cell < ny * y3)
-    w3[:, low:high, :] = g3[0, :, low:high, :] + jnp.where(inside, g3[0, :, 0:1, :], 0.0)
+    w3[:, low:high, :] = g3[:, low:high, :] + jnp.where(inside, g3[:, 0:1, :], 0.0)
 
     def from_w3(x, xs, row, rows):
         return w3[x : x + xs, row : row + rows, :]
@@ -431,91 +593,104 @@
         x, xs = sweep, 8 + x3 - 2 * sweep
         row, rows = low + sweep, high - low - 2 * sweep
         center, applied = block_stencil(
-            from_w3, g3[1, x : x + xs, row : row + rows, :], x, xs, row, rows, 16
+            from_w3, k3[x : x + xs, row : row + rows, :], x, xs, row, rows, 16
         )
-        value = center + g3[0, x : x + xs, row : row + rows, :] - mixed1(T3, applied, 16)
+        value = center + g3[x : x + xs, row : row + rows, :] - mixed1(T3, applied, 16)
         if sweep < 3:
             w3[x : x + xs, row : row + rows, :] = value
         else:
-            b3[:, 0:rows, :] = value
-
-    xs, rows = x3 + 2, y3 + 2
-    children = spread(b3[...].reshape(xs * 8, LANES), last_up[...]).reshape(xs, 8, LANES)
-    for i in range(xs):
-        for s in range(2):
-            q2[i, pl.ds(PAD - 2 + s, rows, stride=2), :] = children[i, 0:rows, :]
-    row, rows = PAD - 2, y2 + 4
-    for i in range(xs):
-        for s in range(2):
-            v2[1 + 2 * i + s, row : row + rows, :] += q2[i, row : row + rows, :]
-    row, rows = PAD - 1, y2 + 2
-    center, applied = block_stencil(
-        from_v2, g2[1, 2 : x2 + 4, row : row + rows, :], 2, x2 + 2, row, rows, 32
-    )
-    w2[:, 0:rows, :] = center + g2[0, 2 : x2 + 4, row : row + rows, :] - mixed1(T2, applied, 32)
-
-    xs = x2 + 2
-    children = spread(w2[...].reshape(xs * 16, LANES), up[...]).reshape(xs, 16, 2 * LANES)
+            b3[:, row : row + rows, :] = value
+
+    below = b3[...]
+    mixed = mixed1(T2_below, below, 16)
+    flat = ((x3 + 2) * 2 * PAD, LANES)
+    e2[...] = spread_stacked((below - mixed).reshape(flat), last_up[...]).reshape(e2.shape)
+    m2[...] = spread_stacked(mixed.reshape(flat), last_rise[...]).reshape(m2.shape)
+    q2[...] = spread_stacked(mixed.reshape(flat), last_up[...]).reshape(q2.shape)
+
+    def raised(m, q, c, i, s, t, row, rows):
+        other_y = q[c, i, row + 2 * t - 1 : row + 2 * t - 1 + rows, :]
+        other_x = q[c, i + 2 * s - 1, row : row + rows, :]
+        return m[c, i, row : row + rows, :] - other_y - other_x
+
+    for x in range(-1, x2 + 1):
+        i, s = x // 2 + 1, x % 2
+        for t in range(2):
+            row, rows = PAD - t, y3 + 1
+            cells = pl.ds(PAD - t, rows, stride=2)
+            value = raised(m2, q2, 0, i, s, t, row, rows)
+            w2[x + 1, cells, :] = (
+                x2_part[x + 1, cells, :]
+                + e2[0, i, row : row + rows, :]
+                - g2[1, x + 3, cells, :] * value
+            )
+
+    below = w2[...]
+    mixed = mixed1(T1_below, below, 32)
+    flat = ((x2 + 2) * (y2 + 2 * PAD), LANES)
+    shape = (x2 + 2, y2 + 2 * PAD, LANES)
+    for field, matrix, target in (
+        (below - mixed, up, e1),
+        (mixed, rise_second, m1),
+        (mixed, up, q1),
+    ):
+        children = spread_stacked(field.reshape(flat), matrix[...])
+        for c in range(2):
+            target[c] = children[:, c * LANES : (c + 1) * LANES].reshape(shape)
+    for x in range(-1, x1 + 1):
+        i, s = x // 2 + 1, x % 2
+        for t in range(2):
+            row, rows = PAD - t, y2 + 1
+            cells = pl.ds(PAD - t, rows, stride=2)
+            coefficient = g1[2, x + 3, cells, :]
+            for c in range(2):
+                value = raised(m1, q1, c, i, s, t, row, rows)
+                w1[c, x + 1, cells, :] = (
+                    x1_part[c, x + 1, cells, :]
+                    + e1[c, i, row : row + rows, :]
+                    - coefficient * value
+                )
+
+    below = [w1[c] for c in range(2)]
+    mixed = mixed2(T0_below, below)
+    own = slice(1, x1 + 1), slice(PAD, PAD + y1)
     for g in range(2):
-        for i in range(xs):
-            for s in range(2):
-                q1[g, i, pl.ds(PAD - 2 + s, rows, stride=2), :] = children[
-                    i, 0:rows, g * LANES : (g + 1) * LANES
-                ]
-
-    def lift_second(step):
-        row, rows = PAD - 2, y1 + 4
-        for g in range(2):
-            part = q1[g, step // 2, row : row + rows, :]
-            v1[g, step + 1, row : row + rows, :] += part
-
-    steps(x1 + 4, lift_second)
-
-    def finish_second(step):
-        x = step + 2
-        row, rows = PAD - 1, y1 + 2
-        coefficient = g1[2, x, row : row + rows, :]
-        change = mixed2(T1, [stencil_of(v1, coefficient, c, x, row, rows, 64) for c in range(2)])
+        inner = (x1 * y1, LANES)
+        for field, matrix, target in (
+            ((below[g] - mixed[g])[own].reshape(inner), up, e0),
+            (mixed[g][own].reshape(inner), rise_fine, m0),
+        ):
+            children = spread_stacked(field, matrix[...])
+            for c in range(2):
+                part = children[:, c * LANES : (c + 1) * LANES]
+                target[2 * g + c, 1 : x1 + 1, PAD : PAD + y1, :] = part.reshape(x1, y1, LANES)
+        children = spread_stacked(
+            mixed[g].reshape((x1 + 2) * (y1 + 2 * PAD), LANES), up[...]
+        )
         for c in range(2):
-            value = v1[c, x, row : row + rows, :] + g1[c, x, row : row + rows, :] - change[c]
-            w1[c, step, 0:rows, :] = value
-
-    steps(x1 + 2, finish_second)
-
-    def spread_fine(i):
-        rows = y1 + 2
-        for g in range(2):
-            children = spread(w1[g, i], up[...])
-            for c in range(2):
+            part = children[:, c * LANES : (c + 1) * LANES]
+            q0[2 * g + c] = part.reshape(x1 + 2, y1 + 2 * PAD, LANES)
+
+    def finish_fine(step):
+        i = step + 1
+        for t in range(2):
+            cells = pl.ds(t, y1, stride=2)
+            coefficient = [a0[2 * step + s + 1, pl.ds(t, y1, stride=2), :] for s in range(2)]
+            for c in range(4):
                 for s in range(2):
-                    q0[2 * g + c, i, pl.ds(PAD - 2 + s, rows, stride=2), :] = children[
-                        0:rows, c * LANES : (c + 1) * LANES
-                    ]
-
-    steps(x1 + 2, spread_fine)
-
-    def lift_fine(step):
-        row, rows = PAD - 1, y0 + 2
-        for c in range(4):
-            part = q0[c, (step + 1) // 2, row : row + rows, :]
-            v0[c, step + 1, row : row + rows, :] += part
-
-    steps(x0 + 2, lift_fine)
-
-    def finish_fine(x):
-        coefficient = g0[4, x + 2, PAD : PAD + y0, :]
-        change = mixed4(
-            T0, [stencil_of(v0, coefficient, c, x + 2, PAD, y0, LANES) for c in range(4)]
-        )
-        for c in range(4):
-            value = v0[c, x + 2, PAD : PAD + y0, :] + g0[c, x + 2, PAD : PAD + y0, :]
-            f0[c, x] = value - change[c]
-
-    quarter = x0 // 4
+                    value = raised(m0, q0, c, i, s, t, PAD, y1)
+                    x = 2 * step + s
+                    f0[c, x, cells, :] = (
+                        f0[c, x, cells, :]
+                        + e0[c, i, PAD : PAD + y1, :]
+                        - coefficient[s] * value
+                    )
+
+    quarter = x1 // 4
     stores = []
     for q in range(4):
         steps(quarter, lambda i, q=q: finish_fine(i + q * quarter))
-        part = pl.ds(q * quarter, quarter)
+        part = pl.ds(2 * q * quarter, 2 * quarter)
         store = pltpu.make_async_copy(f0.at[:, part], out.at[:, part], out_sem.at[q])
         store.start()
         stores.append(store)
@@ -545,31 +720,42 @@
             vmem(4, near, 8, LANES),
         ]
 
+    def three(groups, xs, ys):
+        return [vmem(groups, xs + 2, ys + 2 * PAD, LANES)] * 3
+
+    double = pltpu.VMEM((2 * LANES, 2 * LANES), BF16)
+    tall = pltpu.VMEM((2 * LANES, LANES), BF16)
     scratch = (
-        [vmem(4, x0, y0, LANES), padded(5, x0, y0, 2), padded(4, x0, y0, 2)]
-        + [vmem(4, x1, y0, LANES), vmem(4, x1 + 2, y0 + 2 * PAD, LANES)]
+        [vmem(4, x0, y0, LANES), vmem(x0 + 2, y0, LANES)]
+        + [vmem(4, (x0 + 4) * (y0 + 2 * PAD), LANES)] * 2
+        + [vmem(2, 4, x0 + 2 * PAD, LANES)]
+        + [vmem(4, x1, y0, LANES)]
+        + three(4, x1, y1)
         + faces(9, 4, x0)
         + [vmem(*second.shape), vmem(2, x1, y1, LANES), padded(3, x1, y1, 3), padded(2, x1, y1, 3)]
-        + [vmem(2, x2, y1, LANES), vmem(2, x2 + 2, y1 + 2 * PAD, LANES)]
-        + [vmem(2, x1 + 2, y1 + 8, LANES)]
+        + [vmem(2, x2, y1, LANES), vmem(2, x1 + 2, y1 + 2 * PAD, LANES)]
+        + three(2, x2, y2)
+        + [vmem(2, x1 + 2, y1 + 2 * PAD, LANES)]
         + faces(8, 5, x1)
         + [vmem(*third.shape), vmem(x2, y2, LANES), padded(2, x2, y2, 3)]
         + [vmem(x2 + 6, y2 + 2 * PAD, LANES), vmem(x3, y2, LANES)]
-        + [vmem(x3 + 2, y2 + 2 * PAD, LANES), vmem(x2 + 2, 16, LANES)]
+        + [vmem(x2 + 2, y2 + 2 * PAD, LANES)]
+        + [vmem(1, x3 + 2, 2 * PAD, LANES)] * 3
+        + [vmem(x2 + 2, y2 + 2 * PAD, LANES)]
         + faces(5, 5, x2)
-        + [vmem(*coarse.shape), vmem(x3, y2, LANES), vmem(2, x3 + 8, 24, LANES)]
-        + [vmem(x3 + 8, 24, LANES), vmem(x3 + 2, 8, LANES)]
-        + [vmem(x3, 2 * y3, LANES), vmem(2, x3, 2 * y3, LANES)]
+        + [vmem(*coarse.shape), vmem(x3, y2, LANES)]
+        + [vmem(x3 + 8, 24, LANES)] * 3
+        + [vmem(x3 + 2, 2 * PAD, LANES)]
+        + [vmem(x3 * y3, LANES), vmem(2, x3 * y3, LANES)] * 2
         + [vmem(x3, LANES), vmem(ny - 1, x3, LANES)]
-        + [vmem(48, LANES)]
-        + [pltpu.VMEM((2 * LANES, LANES), BF16), pltpu.VMEM((LANES, 2 * LANES), BF16)]
-        + [pltpu.VMEM((LANES, LANES), BF16), pltpu.VMEM((LANES, LANES), BF16)]
+        + [vmem(64, LANES)]
+        + [tall, double, double, double, pltpu.VMEM((LANES, LANES), BF16), tall, tall]
     )
-    copies = 8 * 3 + 2 + (ny - 1) + 4
+    copies = 8 * 3 + 4 + 2 * 2 + (ny - 1) + 4 * 2
     scratch += [
         pltpu.SemaphoreType.DMA((copies,)),
         pltpu.SemaphoreType.DMA((copies,)),
-        pltpu.SemaphoreType.DMA((5,)),
+        pltpu.SemaphoreType.DMA((7,)),
         pltpu.SemaphoreType.DMA((4,)),
     ]
     anywhere = pl.BlockSpec(memory_space=pl.ANY)
@@ -581,7 +767,7 @@
         out_specs=anywhere,
         scratch_shapes=scratch,
         compiler_params=pltpu.CompilerParams(
-            collective_id=0, has_side_effects=True, vmem_limit_bytes=40 * 1024 * 1024
+            collective_id=0, has_side_effects=True, vmem_limit_bytes=60 * 1024 * 1024
         ),
     )(source, fine, second, third, coarse, mixers, smoothers)
 

time: 71.9 us -> 60.2 us (0.84)
  Pallas kernels: 64.7 us -> 57.7 us
  local copies, waits for them, and re-layouts: 6.78 us -> 2.26 us
    pallas_call x1, Pallas kernels: 64.7 us -> 57.7 us  [per_device(): pl.pallas_call(functools.partial(kernel, nx, ny), out_shape=jax.ShapeDtyp...]
    unnamed x15 -> x1, local copies, waits for them, and re-layouts: 6.78 us -> 2.26 us
where the time goes in v1:
time: 60.2 us; the launch traced here: 60 us
  Pallas kernels  57.7 us (96%)
  local copies, waits for them, and re-layouts  2.26 us (4%)
    pallas_call x1, Pallas kernels, per_device(): pl.pallas_call(functools.partial(kernel, nx, ny), out_shape=jax.ShapeDtyp...  57.7 us
    unnamed x1, local copies, waits for them, and re-layouts  2.26 us

profile of v1, /device:TPU:1, one launch (start us, length us, event | category | flops | bytes accessed | tf_op | source)
XLA Modules:
  0.0 60.0 jit_solution(3010253425648235076)
XLA Ops:
  0.0 57.7 %shard_map.73 = f32[4,16,32,128]{3,2,1,0:T(8,128)} custom-call(f32[4,16,32,128]{3,2,1,0:T(8,128)} %source.1, f32[16,32,128]{2,1,0:T(8,128)} %fine.1, f32[8,16,64]{2,1,0:T(8,128)} %second.1, f32[4,8,32]{2,1,0:T(8,128)} %third.1, f32[2,4,16]{2,1,0:T(4,128)} %coarse.1, f32[4,4,4]{2,1,0:T(4,128)} %mixers.1, f32[4,4,4]{2,1,0:T(4,128)} %smoothers.1), custom_call_target="tpu_custom_call" | custom-call | tf_op jit(solution)/shard_map/pallas_call | solution.py:763
  57.7 2.3 %copy.9 = f32[4,16,32,128]{3,2,1,0:T(8,128)} copy(f32[4,16,32,128]{3,2,1,0:T(8,128)} %shard_map.73) | data formatting | bytes 2097152

commit v2 on v1

--- a/solution.py
+++ b/solution.py
@@ -48,13 +48,13 @@
 
 def kernel(
     nx, ny,
-    source, fine, second, third, coarse, mixers, smoothers, out,
+    source, fine, second, third, coarse, mixers_in, smoothers_in, out,
     f0, a0, g0, v0, h0, r0, e0, m0, q0, s0, p0, c0,
     a1, f1, g1, v1, r1, x1_part, e1, m1, q1, w1, s1, p1, c1,
     a2, f2, g2, v2, r2, x2_part, e2, m2, q2, w2, s2, p2, c2,
     a3, r3, g3, k3, w3, b3, s3, p3, t3, u3, line, lines,
     table, down, up, rise_fine, rise_second, last_down, last_up, last_rise,
-    send_sem, recv_sem, local_sem, out_sem,
+    mixers, smoothers, send_sem, recv_sem, local_sem,
 ):
     mx, my = lax.axis_index("gx"), lax.axis_index("gy")
 
@@ -64,9 +64,6 @@
     barrier = pltpu.get_barrier_semaphore()
     peers = [(0, k) for k in range(1, ny)]
     peers += [(dx, dy) for dx in (-1, 1) for dy in (-1, 0, 1)] + [(-2, 0), (2, 0)]
-    for dx, dy in peers:
-        pl.semaphore_signal(barrier, inc=1, device_id=device(dx, dy), device_id_type=MESH)
-
     x0, y0 = f0.shape[1:3]
     x1, y1 = f1.shape[1:3]
     x2, y2 = f2.shape[:2]
@@ -85,8 +82,12 @@
         pltpu.make_async_copy(third, a2, local_sem.at[2]),
         pltpu.make_async_copy(coarse, a3, local_sem.at[3]),
     ]
-    for load in load_parts + [load_fine] + load_coarser:
+    load_smoothers = pltpu.make_async_copy(smoothers_in, smoothers, local_sem.at[7])
+    load_mixers = pltpu.make_async_copy(mixers_in, mixers, local_sem.at[8])
+    for load in [load_smoothers] + load_parts + [load_fine, load_mixers] + load_coarser:
         load.start()
+    for dx, dy in peers:
+        pl.semaphore_signal(barrier, inc=1, device_id=device(dx, dy), device_id_type=MESH)
 
     def smooth_matrix(level):
         return [
@@ -141,6 +142,7 @@
             rows.append(keep(vector))
         return rows
 
+    load_smoothers.wait()
     S0 = smooth_matrix(0)
 
     def mixed4(matrix, fields):
@@ -220,10 +222,11 @@
         copies = [
             send(g.at[:, pl.ds(xs, h), own], g.at[:, pl.ds(0, h), own], (1, 0)),
             send(g.at[:, pl.ds(h, h), own], g.at[:, pl.ds(xs + h, h), own], (-1, 0)),
-            send(s.at[1], p.at[0], (0, 1)),
-            send(s.at[0], p.at[1], (0, -1)),
-        ]
-        return copies + send_corners(s, corner, xs, near)
+        ]
+        copies += send_corners(s, corner, xs, near)
+        copies.append(send(s.at[1], p.at[0], (0, 1)))
+        copies.append(send(s.at[0], p.at[1], (0, -1)))
+        return copies
 
     def unpack(copies, g, p, corner, planes, h, xs, ys, near, reach, a_reach):
         for copy in copies:
@@ -321,13 +324,14 @@
             s0[1, n] = g0[c, fine_plane(PAD + y0 - 1 - k), :]
     s0[0, 4] = a0[1 : x0 + 1, 0, :]
     s0[1, 4] = a0[1 : x0 + 1, y0 - 1, :]
+    copies += send_corners(s0, c0, x0, 4)
     copies.append(send(s0.at[1], p0.at[0], (0, 1)))
     copies.append(send(s0.at[0], p0.at[1], (0, -1)))
-    copies += send_corners(s0, c0, x0, 4)
 
     for c in range(4):
         for row in (PAD - 1, PAD + y0):
             g0[c, fine_plane(row), :] = jnp.zeros((x0, LANES), F32)
+    load_mixers.wait()
     B0 = mix_matrix(0)
     T0 = product(S0, B0)
 
@@ -680,24 +684,15 @@
                 for s in range(2):
                     value = raised(m0, q0, c, i, s, t, PAD, y1)
                     x = 2 * step + s
-                    f0[c, x, cells, :] = (
+                    out[c, x, cells, :] = (
                         f0[c, x, cells, :]
                         + e0[c, i, PAD : PAD + y1, :]
                         - coefficient[s] * value
                     )
 
-    quarter = x1 // 4
-    stores = []
-    for q in range(4):
-        steps(quarter, lambda i, q=q: finish_fine(i + q * quarter))
-        part = pl.ds(2 * q * quarter, 2 * quarter)
-        store = pltpu.make_async_copy(f0.at[:, part], out.at[:, part], out_sem.at[q])
-        store.start()
-        stores.append(store)
+    steps(x1, finish_fine)
     for copy in started:
         copy.wait_send()
-    for store in stores:
-        store.wait()
 
 
 def per_device(nx, ny, source, fine, second, third, coarse, mixers, smoothers):
@@ -753,21 +748,21 @@
     )
     copies = 8 * 3 + 4 + 2 * 2 + (ny - 1) + 4 * 2
     scratch += [
+        pltpu.SMEM(mixers.shape, F32),
+        pltpu.SMEM(smoothers.shape, F32),
         pltpu.SemaphoreType.DMA((copies,)),
         pltpu.SemaphoreType.DMA((copies,)),
-        pltpu.SemaphoreType.DMA((7,)),
-        pltpu.SemaphoreType.DMA((4,)),
+        pltpu.SemaphoreType.DMA((9,)),
     ]
     anywhere = pl.BlockSpec(memory_space=pl.ANY)
-    scalars = pl.BlockSpec(memory_space=pltpu.SMEM)
     return pl.pallas_call(
         functools.partial(kernel, nx, ny),
-        out_shape=jax.ShapeDtypeStruct(source.shape, F32),
-        in_specs=[anywhere] * 5 + [scalars] * 2,
-        out_specs=anywhere,
+        out_shape=pltpu.VMEM(source.shape, F32),
+        in_specs=[anywhere] * 7,
+        out_specs=pl.BlockSpec(memory_space=pltpu.VMEM),
         scratch_shapes=scratch,
         compiler_params=pltpu.CompilerParams(
-            collective_id=0, has_side_effects=True, vmem_limit_bytes=60 * 1024 * 1024
+            collective_id=0, has_side_effects=True, vmem_limit_bytes=56 * 1024 * 1024
         ),
     )(source, fine, second, third, coarse, mixers, smoothers)
 

time: 60.2 us -> 55.8 us (0.927)
  Pallas kernels: 57.7 us -> 54.7 us
  local copies, waits for them, and re-layouts: 2.26 us -> 0.97 us
    pallas_call x1, Pallas kernels: 57.7 us -> 54.7 us  [per_device(): pl.pallas_call(functools.partial(kernel, nx, ny), out_shape=pltpu.VMEM(so...]
    unnamed x1, local copies, waits for them, and re-layouts: 2.26 us -> 0.97 us
where the time goes in v2:
time: 55.8 us; the launch traced here: 55.7 us
  Pallas kernels  54.7 us (98%)
  local copies, waits for them, and re-layouts  0.97 us (2%)
    pallas_call x1, Pallas kernels, per_device(): pl.pallas_call(functools.partial(kernel, nx, ny), out_shape=pltpu.VMEM(so...  54.7 us

profile of v2, /device:TPU:1, one launch (start us, length us, event | category | flops | bytes accessed | tf_op | source)
XLA Modules:
  0.0 55.7 jit_solution(17357073796585893150)
XLA Ops:
  0.0 54.7 %shard_map.73 = f32[4,16,32,128]{3,2,1,0:T(8,128)S(1)} custom-call(f32[4,16,32,128]{3,2,1,0:T(8,128)} %source.1, f32[16,32,128]{2,1,0:T(8,128)} %fine.1, f32[8,16,64]{2,1,0:T(8,128)} %second.1, f32[4,8,32]{2,1,0:T(8,128)} %third.1, f32[2,4,16]{2,1,0:T(4,128)} %coarse.1, f32[4,4,4]{2,1,0:T(4,128)} %mixers_in.1, f32[4,4,4]{2,1,0:T(4,128)} %smoothers_in.1), custom_call_target="tpu_custom_call" | custom-call | tf_op jit(solution)/shard_map/pallas_call | solution.py:758
  54.7 1.0 %copy.9 = f32[4,16,32,128]{3,2,1,0:T(8,128)} copy(f32[4,16,32,128]{3,2,1,0:T(8,128)S(1)} %shard_map.73) | data formatting | bytes 2097152

commit v3 on v2

--- a/solution.py
+++ b/solution.py
@@ -49,10 +49,10 @@
 def kernel(
     nx, ny,
     source, fine, second, third, coarse, mixers_in, smoothers_in, out,
-    f0, a0, g0, v0, h0, r0, e0, m0, q0, s0, p0, c0,
-    a1, f1, g1, v1, r1, x1_part, e1, m1, q1, w1, s1, p1, c1,
-    a2, f2, g2, v2, r2, x2_part, e2, m2, q2, w2, s2, p2, c2,
-    a3, r3, g3, k3, w3, b3, s3, p3, t3, u3, line, lines,
+    fx, f0, a0, g0, v0, h0, r0, e0, m0, q0, s0, p0, d0, c0,
+    a1, f1, g1, v1, r1, x1_part, e1, m1, q1, w1, s1, p1, d1, c1,
+    a2, f2, g2, v2, r2, x2_part, e2, m2, q2, w2, s2, p2, d2, c2,
+    a3, r3, g3, k3, w3, b3, s3, p3, t3, u3, b_k3, l_k3, b_g3, l_g3, line, lines,
     table, down, up, rise_fine, rise_second, last_down, last_up, last_rise,
     mixers, smoothers, send_sem, recv_sem, local_sem,
 ):
@@ -68,8 +68,8 @@
     x1, y1 = f1.shape[1:3]
     x2, y2 = f2.shape[:2]
     x3, y3 = a3.shape[:2]
-    first_rows = min(4, x0 // 4)
-    parts = [(0, first_rows), (x0 - first_rows, first_rows), (first_rows, x0 - 2 * first_rows)]
+    part_rows = x0 // 4
+    parts = [(n * part_rows, part_rows) for n in range(4)]
     load_fine = pltpu.make_async_copy(fine, a0.at[pl.ds(1, x0)], local_sem.at[0])
     load_parts = [
         pltpu.make_async_copy(
@@ -82,8 +82,8 @@
         pltpu.make_async_copy(third, a2, local_sem.at[2]),
         pltpu.make_async_copy(coarse, a3, local_sem.at[3]),
     ]
-    load_smoothers = pltpu.make_async_copy(smoothers_in, smoothers, local_sem.at[7])
-    load_mixers = pltpu.make_async_copy(mixers_in, mixers, local_sem.at[8])
+    load_smoothers = pltpu.make_async_copy(smoothers_in, smoothers, local_sem.at[8])
+    load_mixers = pltpu.make_async_copy(mixers_in, mixers, local_sem.at[9])
     for load in [load_smoothers] + load_parts + [load_fine, load_mixers] + load_coarser:
         load.start()
     for dx, dy in peers:
@@ -203,45 +203,46 @@
             s[0, p, 0:xs, :] = g[c, h : h + xs, PAD + k, :]
             s[1, p, 0:xs, :] = g[c, h : h + xs, PAD + ys - 1 - k, :]
 
-    def send_corners(s, corner, xs, near):
+    def corner_cells(planes, reach_of):
+        return [
+            (n, i) for n, (k, c) in enumerate(planes) for i in range(reach_of(c) - 1 - k)
+        ]
+
+    def send_corners(s, packed, corner, cells, xs):
         copies = []
-        first, last = pl.ds(0, 8), pl.ds(max(xs - 8, 0), 8)
         for side, dy in ((1, 1), (0, -1)):
-            for end, dx in ((last, 1), (first, -1)):
-                copies.append(
-                    send(
-                        s.at[side, pl.ds(0, near), end],
-                        corner.at[(0 if dx > 0 else 1) * 2 + (0 if dy > 0 else 1)],
-                        (dx, dy),
-                    )
-                )
+            for dx in (1, -1):
+                slot = (0 if dx > 0 else 1) * 2 + (0 if dy > 0 else 1)
+                for r, (n, i) in enumerate(cells):
+                    x = xs - 1 - i if dx > 0 else i
+                    packed[slot, r : r + 1, :] = s[side, n, x : x + 1, :]
+                copies.append(send(packed.at[slot], corner.at[slot], (dx, dy)))
         return copies
 
-    def exchange(g, s, p, corner, h, xs, ys, near):
+    def exchange(g, s, p, packed, corner, cells, h, xs, ys):
         own = pl.ds(PAD, ys)
         copies = [
             send(g.at[:, pl.ds(xs, h), own], g.at[:, pl.ds(0, h), own], (1, 0)),
             send(g.at[:, pl.ds(h, h), own], g.at[:, pl.ds(xs + h, h), own], (-1, 0)),
         ]
-        copies += send_corners(s, corner, xs, near)
+        copies += send_corners(s, packed, corner, cells, xs)
         copies.append(send(s.at[1], p.at[0], (0, 1)))
         copies.append(send(s.at[0], p.at[1], (0, -1)))
         return copies
 
-    def unpack(copies, g, p, corner, planes, h, xs, ys, near, reach, a_reach):
+    def unpack(copies, g, p, corner, cells, planes, h, xs, ys):
         for copy in copies:
             copy.wait_recv()
         groups = g.shape[0]
         for n, (k, c) in enumerate(planes):
             g[c, h : h + xs, PAD - 1 - k, :] = p[0, n, 0:xs, :]
             g[c, h : h + xs, PAD + ys + k, :] = p[1, n, 0:xs, :]
-        top = min(xs, 8) - 1
-        for n, (k, c) in enumerate(planes[:near]):
-            for i in range((a_reach if c == groups - 1 else reach) - 1 - k):
-                for from_dy in range(2):
-                    row = PAD - 1 - k if from_dy == 0 else PAD + ys + k
-                    g[c, h - 1 - i, row : row + 1, :] = corner[from_dy, n, top - i : top - i + 1, :]
-                    g[c, h + xs + i, row : row + 1, :] = corner[2 + from_dy, n, i : i + 1, :]
+        for r, (n, i) in enumerate(cells):
+            k, c = planes[n]
+            for from_dy in range(2):
+                row = PAD - 1 - k if from_dy == 0 else PAD + ys + k
+                g[c, h - 1 - i, row : row + 1, :] = corner[from_dy, r : r + 1, :]
+                g[c, h + xs + i, row : row + 1, :] = corner[2 + from_dy, r : r + 1, :]
 
         @pl.when(mx == 0)
         def _():
@@ -301,22 +302,16 @@
         x, xs = parts[n]
         steps(xs, lambda i: smooth_fine(i + x))
 
-    smooth_part(0)
-    smooth_part(1)
+    pl.semaphore_wait(barrier, len(peers))
+    copies = [
+        send(source.at[:, pl.ds(x0 - 2, 2)], fx.at[0], (1, 0)),
+        send(source.at[:, pl.ds(0, 2)], fx.at[1], (-1, 0)),
+        send(fine.at[pl.ds(x0 - 1, 1)], a0.at[pl.ds(0, 1)], (1, 0)),
+        send(fine.at[pl.ds(0, 1)], a0.at[pl.ds(x0 + 1, 1)], (-1, 0)),
+    ]
+    for n in range(len(parts)):
+        smooth_part(n)
     load_fine.wait()
-    pl.semaphore_wait(barrier, len(peers))
-    copies = []
-    for layer, dst, dx in ((x0 + 1, 1, 1), (2, x0 + 2, -1), (x0, 0, 1), (3, x0 + 3, -1)):
-        copies.append(
-            send(
-                g0.at[:, pl.ds(layer * y_rows + PAD, y0)],
-                g0.at[:, pl.ds(dst * y_rows + PAD, y0)],
-                (dx, 0),
-            )
-        )
-    copies.append(send(a0.at[pl.ds(x0, 1)], a0.at[pl.ds(0, 1)], (1, 0)))
-    copies.append(send(a0.at[pl.ds(1, 1)], a0.at[pl.ds(x0 + 1, 1)], (-1, 0)))
-    smooth_part(2)
     for c in range(4):
         for k in range(2):
             n = c if k == 0 else 5 + c
@@ -324,7 +319,7 @@
             s0[1, n] = g0[c, fine_plane(PAD + y0 - 1 - k), :]
     s0[0, 4] = a0[1 : x0 + 1, 0, :]
     s0[1, 4] = a0[1 : x0 + 1, y0 - 1, :]
-    copies += send_corners(s0, c0, x0, 4)
+    copies += send_corners(s0, d0, c0, [(c, 0) for c in range(4)], x0)
     copies.append(send(s0.at[1], p0.at[0], (0, 1)))
     copies.append(send(s0.at[0], p0.at[1], (0, -1)))
 
@@ -377,6 +372,14 @@
     for copy in copies:
         copy.wait_recv()
 
+    def smooth_beside(i):
+        fields = mixed4(S0, [fx[i // 2, c, i % 2] for c in range(4)])
+        for c in range(4):
+            start = pl.multiple_of((i + x0 * (i // 2)) * y_rows + PAD, 8)
+            g0[c, pl.ds(start, y0), :] = fields[c]
+
+    steps(4, smooth_beside)
+
     @pl.when(mx == 0)
     def _():
         g0[:, 0 : 2 * y_rows] = jnp.zeros((4, 2 * y_rows, LANES), F32)
@@ -399,7 +402,7 @@
 
     for c in range(4):
         for side, row in ((0, PAD - 1), (1, PAD + y0)):
-            left, right = c0[side, c, 7:8, :], c0[2 + side, c, 0:1, :]
+            left, right = c0[side, c : c + 1, :], c0[2 + side, c : c + 1, :]
             g0[c, y_rows + row : y_rows + row + 1, :] = left
             g0[c, (x0 + 2) * y_rows + row : (x0 + 2) * y_rows + row + 1, :] = right
             h0[side, c, PAD - 1 : PAD, :] = left
@@ -444,8 +447,9 @@
     for g in range(2):
         g1[g, 3 : 3 + x1, PAD : PAD + y1, :] = fields[g]
     planes1 = [(0, 0), (0, 1), (0, 2), (1, 0), (1, 1), (1, 2), (2, 0), (2, 1)]
+    cells1 = corner_cells(planes1, lambda c: 2 if c == 2 else 3)
     pack(g1, s1, planes1, 3, x1, y1)
-    copies = exchange(g1, s1, p1, c1, 3, x1, y1, 5)
+    copies = exchange(g1, s1, p1, d1, c1, cells1, 3, x1, y1)
 
     def fill_beside(buffer, received):
         for side, row in ((0, PAD - y3), (1, PAD + y3)):
@@ -455,27 +459,31 @@
                     inside, received[side, x * y3 : (x + 1) * y3, :], 0.0
                 )
 
-    def send_block(buffer):
-        block, used = pl.ds(4, x3), pl.ds(0, 2 * PAD)
-        return [
-            send(buffer.at[block, used], buffer.at[pl.ds(4 - dx * x3, x3), used], (dx, 0))
-            for dx in (1, -1, 2, -2)
-        ]
-
-    def receive_block(buffer, copies):
+    first_half = lane < 64
+    block_steps = (2, -2, 1, -1)
+
+    def send_block(buffer, packed, received):
+        rows = slice(0, 2 * PAD)
+        packed[...] = jnp.where(first_half, buffer[4, rows, :], buffer[5, rows, :])
+        return [
+            send(packed, received.at[n], (dx, 0)) for n, dx in enumerate(block_steps)
+        ]
+
+    def receive_block(buffer, received, copies):
         for copy in copies:
             copy.wait_recv()
-        for dx in (1, -1, 2, -2):
+        for n, dx in enumerate(block_steps):
             outside = (mx < dx) if dx > 0 else (mx >= nx + dx)
-
-            @pl.when(outside)
-            def _(dx=dx):
-                buffer[4 - dx * x3 : 4 - dx * x3 + x3] = jnp.zeros((x3,) + buffer.shape[1:], F32)
+            block = jnp.where(outside, 0.0, received[n])
+            turned = pltpu.roll(block, 64, 1)
+            x = 4 - 2 * dx
+            buffer[x, 0 : 2 * PAD, :] = jnp.where(first_half, block, turned)
+            buffer[x + 1, 0 : 2 * PAD, :] = jnp.where(first_half, turned, block)
 
     for copy in coarse_copies:
         copy.wait_recv()
     fill_beside(k3, u3)
-    coarse_copies = send_block(k3)
+    coarse_copies = send_block(k3, b_k3, l_k3)
 
     def settle_fine(x):
         change = mixed4(T0, [fine_stencil(v0, a0[x + 1], c, x + 2) for c in range(4)])
@@ -484,7 +492,7 @@
             f0[c, x] = value - change[c]
 
     steps(x0, settle_fine)
-    unpack(copies, g1, p1, c1, planes1, 3, x1, y1, 5, 3, 2)
+    unpack(copies, g1, p1, c1, cells1, planes1, 3, x1, y1)
 
     def relax_second(step):
         x = step + 1
@@ -519,9 +527,10 @@
     f2[...] = spread(joined, down[...]).reshape(x2, y2, LANES)
     g2[0, 3 : 3 + x2, PAD : PAD + y2, :] = mixed1(S2, f2[...], 32)
     planes2 = [(0, 0), (0, 1), (1, 0), (1, 1), (2, 0)]
+    cells2 = corner_cells(planes2, lambda c: 3 if c == 1 else 4)
     pack(g2, s2, planes2, 3, x2, y2)
-    copies = exchange(g2, s2, p2, c2, 3, x2, y2, 5)
-    receive_block(k3, coarse_copies)
+    copies = exchange(g2, s2, p2, d2, c2, cells2, 3, x2, y2)
+    receive_block(k3, l_k3, coarse_copies)
 
     def settle_second(step):
         x = step + 2
@@ -533,7 +542,7 @@
             x1_part[c, step, row : row + rows, :] = value
 
     steps(x1 + 2, settle_second)
-    unpack(copies, g2, p2, c2, planes2, 3, x2, y2, 5, 4, 3)
+    unpack(copies, g2, p2, c2, cells2, planes2, 3, x2, y2)
 
     def block_stencil(load, coefficient, x, xs, row, rows, segment):
         center = load(x, xs, row, rows)
@@ -583,7 +592,7 @@
     for x in range(x3):
         g3[4 + x, 0:1, :] = total[x : x + 1, :]
     fill_beside(g3, p3)
-    receive_block(g3, send_block(g3))
+    receive_block(g3, l_g3, send_block(g3, b_g3, l_g3))
 
     low, high = PAD - y3, PAD + 2 * y3
     cell = lax.broadcasted_iota(jnp.int32, (1, 3 * y3, LANES), 1) + (my - 1) * y3
@@ -712,7 +721,8 @@
         return [
             vmem(2, planes, rows, LANES),
             vmem(2, planes, rows, LANES),
-            vmem(4, near, 8, LANES),
+            vmem(4, near, LANES),
+            vmem(4, near, LANES),
         ]
 
     def three(groups, xs, ys):
@@ -721,27 +731,28 @@
     double = pltpu.VMEM((2 * LANES, 2 * LANES), BF16)
     tall = pltpu.VMEM((2 * LANES, LANES), BF16)
     scratch = (
-        [vmem(4, x0, y0, LANES), vmem(x0 + 2, y0, LANES)]
+        [vmem(2, 4, 2, y0, LANES), vmem(4, x0, y0, LANES), vmem(x0 + 2, y0, LANES)]
         + [vmem(4, (x0 + 4) * (y0 + 2 * PAD), LANES)] * 2
         + [vmem(2, 4, x0 + 2 * PAD, LANES)]
         + [vmem(4, x1, y0, LANES)]
         + three(4, x1, y1)
-        + faces(9, 4, x0)
+        + faces(9, 8, x0)
         + [vmem(*second.shape), vmem(2, x1, y1, LANES), padded(3, x1, y1, 3), padded(2, x1, y1, 3)]
         + [vmem(2, x2, y1, LANES), vmem(2, x1 + 2, y1 + 2 * PAD, LANES)]
         + three(2, x2, y2)
         + [vmem(2, x1 + 2, y1 + 2 * PAD, LANES)]
-        + faces(8, 5, x1)
+        + faces(8, 8, x1)
         + [vmem(*third.shape), vmem(x2, y2, LANES), padded(2, x2, y2, 3)]
         + [vmem(x2 + 6, y2 + 2 * PAD, LANES), vmem(x3, y2, LANES)]
         + [vmem(x2 + 2, y2 + 2 * PAD, LANES)]
         + [vmem(1, x3 + 2, 2 * PAD, LANES)] * 3
         + [vmem(x2 + 2, y2 + 2 * PAD, LANES)]
-        + faces(5, 5, x2)
+        + faces(5, 16, x2)
         + [vmem(*coarse.shape), vmem(x3, y2, LANES)]
         + [vmem(x3 + 8, 24, LANES)] * 3
         + [vmem(x3 + 2, 2 * PAD, LANES)]
         + [vmem(x3 * y3, LANES), vmem(2, x3 * y3, LANES)] * 2
+        + [vmem(2 * PAD, LANES), vmem(4, 2 * PAD, LANES)] * 2
         + [vmem(x3, LANES), vmem(ny - 1, x3, LANES)]
         + [vmem(64, LANES)]
         + [tall, double, double, double, pltpu.VMEM((LANES, LANES), BF16), tall, tall]
@@ -752,7 +763,7 @@
         pltpu.SMEM(smoothers.shape, F32),
         pltpu.SemaphoreType.DMA((copies,)),
         pltpu.SemaphoreType.DMA((copies,)),
-        pltpu.SemaphoreType.DMA((9,)),
+        pltpu.SemaphoreType.DMA((10,)),
     ]
     anywhere = pl.BlockSpec(memory_space=pl.ANY)
     return pl.pallas_call(

time: 55.8 us -> 54.7 us (0.980)
  Pallas kernels: 54.7 us -> 53.6 us
    pallas_call x1, Pallas kernels: 54.7 us -> 53.6 us  [per_device(): pl.pallas_call(functools.partial(kernel, nx, ny), out_shape=pltpu.VMEM(so...]
where the time goes in v3:
time: 54.7 us; the launch traced here: 54.5 us
  Pallas kernels  53.6 us (98%)
  local copies, waits for them, and re-layouts  0.97 us (2%)
    pallas_call x1, Pallas kernels, per_device(): pl.pallas_call(functools.partial(kernel, nx, ny), out_shape=pltpu.VMEM(so...  53.6 us

profile of v3, /device:TPU:1, one launch (start us, length us, event | category | flops | bytes accessed | tf_op | source)
XLA Modules:
  0.0 54.5 jit_solution(13542738364413425377)
XLA Ops:
  0.0 53.6 %shard_map.73 = f32[4,16,32,128]{3,2,1,0:T(8,128)S(1)} custom-call(f32[4,16,32,128]{3,2,1,0:T(8,128)} %source.1, f32[16,32,128]{2,1,0:T(8,128)} %fine.1, f32[8,16,64]{2,1,0:T(8,128)} %second.1, f32[4,8,32]{2,1,0:T(8,128)} %third.1, f32[2,4,16]{2,1,0:T(4,128)} %coarse.1, f32[4,4,4]{2,1,0:T(4,128)} %mixers_in.1, f32[4,4,4]{2,1,0:T(4,128)} %smoothers_in.1), custom_call_target="tpu_custom_call" | custom-call | tf_op jit(solution)/shard_map/pallas_call | solution.py:769
  53.6 1.0 %copy.9 = f32[4,16,32,128]{3,2,1,0:T(8,128)} copy(f32[4,16,32,128]{3,2,1,0:T(8,128)S(1)} %shard_map.73) | data formatting | bytes 2097152

commit v4 on v3

--- a/solution.py
+++ b/solution.py
@@ -49,7 +49,7 @@
 def kernel(
     nx, ny,
     source, fine, second, third, coarse, mixers_in, smoothers_in, out,
-    fx, f0, a0, g0, v0, h0, r0, e0, m0, q0, s0, p0, d0, c0,
+    fx, o0, f0, a0, g0, v0, h0, r0, e0, m0, q0, s0, p0, d0, c0,
     a1, f1, g1, v1, r1, x1_part, e1, m1, q1, w1, s1, p1, d1, c1,
     a2, f2, g2, v2, r2, x2_part, e2, m2, q2, w2, s2, p2, d2, c2,
     a3, r3, g3, k3, w3, b3, s3, p3, t3, u3, b_k3, l_k3, b_g3, l_g3, line, lines,
@@ -142,8 +142,6 @@
             rows.append(keep(vector))
         return rows
 
-    load_smoothers.wait()
-    S0 = smooth_matrix(0)
 
     def mixed4(matrix, fields):
         return [
@@ -285,10 +283,11 @@
     def fine_plane(row):
         return pl.ds(2 * y_rows + row, x0, stride=y_rows)
 
-    def fine_stencil(buffer, coefficient, c, x):
-        center = fine_rows(buffer, c, x, PAD, y0)
-        beside = fine_rows(buffer, c, x - 1, PAD, y0) + fine_rows(buffer, c, x + 1, PAD, y0)
-        beside += fine_rows(buffer, c, x, PAD - 1, y0) + fine_rows(buffer, c, x, PAD + 1, y0)
+    def fine_stencil(buffer, coefficient, c, x, first=0, count=y0):
+        row = PAD + first
+        center = fine_rows(buffer, c, x, row, count)
+        beside = fine_rows(buffer, c, x - 1, row, count) + fine_rows(buffer, c, x + 1, row, count)
+        beside += fine_rows(buffer, c, x, row - 1, count) + fine_rows(buffer, c, x, row + 1, count)
         return stencil(center, beside, coefficient, LANES)
 
     def smooth_fine(x):
@@ -296,11 +295,6 @@
         for c in range(4):
             start = pl.multiple_of((x + 2) * y_rows + PAD, 8)
             g0[c, pl.ds(start, y0), :] = fields[c]
-
-    def smooth_part(n):
-        load_parts[n].wait()
-        x, xs = parts[n]
-        steps(xs, lambda i: smooth_fine(i + x))
 
     pl.semaphore_wait(barrier, len(peers))
     copies = [
@@ -309,19 +303,27 @@
         send(fine.at[pl.ds(x0 - 1, 1)], a0.at[pl.ds(0, 1)], (1, 0)),
         send(fine.at[pl.ds(0, 1)], a0.at[pl.ds(x0 + 1, 1)], (-1, 0)),
     ]
-    for n in range(len(parts)):
-        smooth_part(n)
+    for load in load_parts:
+        load.wait()
     load_fine.wait()
     for c in range(4):
         for k in range(2):
             n = c if k == 0 else 5 + c
-            s0[0, n] = g0[c, fine_plane(PAD + k), :]
-            s0[1, n] = g0[c, fine_plane(PAD + y0 - 1 - k), :]
+            s0[0, n] = f0[c, :, k, :]
+            s0[1, n] = f0[c, :, y0 - 1 - k, :]
     s0[0, 4] = a0[1 : x0 + 1, 0, :]
     s0[1, 4] = a0[1 : x0 + 1, y0 - 1, :]
     copies += send_corners(s0, d0, c0, [(c, 0) for c in range(4)], x0)
     copies.append(send(s0.at[1], p0.at[0], (0, 1)))
     copies.append(send(s0.at[0], p0.at[1], (0, -1)))
+
+    load_smoothers.wait()
+    S0 = smooth_matrix(0)
+    steps(x0, smooth_fine)
+    for side in range(2):
+        fields = mixed4(S0, [s0[side, c] for c in range(4)])
+        for c in range(4):
+            o0[side, c] = fields[c]
 
     for c in range(4):
         for row in (PAD - 1, PAD + y0):
@@ -338,6 +340,23 @@
             v0[c, pl.ds(pl.multiple_of(x * y_rows + PAD, 8), y0), :] = value
 
     steps(x0 - 2, lambda i: relax_fine(i + 3))
+
+    def residual_fine(i, first, count):
+        total = [None] * 4
+        window = slice(first, first + count)
+        for s in range(2):
+            x = 2 * i + s
+            coefficient = a0[x + 1, window, :]
+            applied = mixed4(
+                B0, [fine_stencil(v0, coefficient, c, x + 2, first, count) for c in range(4)]
+            )
+            for c in range(4):
+                rest = f0[c, x, window, :] - applied[c]
+                total[c] = rest if s == 0 else total[c] + rest
+        for c in range(4):
+            r0[c, i, window, :] = total[c]
+
+    steps(x1 - 2, lambda i: residual_fine(i + 1, 8, y0 - 16))
     for load in load_coarser:
         load.wait()
     third_cells = jnp.concatenate([a3[...]] * 8, axis=-1)
@@ -379,6 +398,15 @@
             g0[c, pl.ds(start, y0), :] = fields[c]
 
     steps(4, smooth_beside)
+    for side in range(2):
+        for first in (0, 5):
+            fields = mixed4(S0, [p0[side, first + c] for c in range(4)])
+            for c in range(4):
+                p0[side, first + c] = fields[c]
+    for slot in range(4):
+        fields = mixed4(S0, [c0[slot, c : c + 1, :] for c in range(4)])
+        for c in range(4):
+            c0[slot, c : c + 1, :] = fields[c]
 
     @pl.when(mx == 0)
     def _():
@@ -417,24 +445,15 @@
         applied = []
         for c in range(4):
             beside = h0[side, c, PAD - 1 : PAD - 1 + x0, :] + h0[side, c, PAD + 1 : PAD + 1 + x0, :]
-            beside += p0[side, 5 + c] + s0[side, c]
+            beside += p0[side, 5 + c] + o0[side, c]
             applied.append(stencil(near[c], beside, p0[side, 4], LANES))
         change = mixed4(T0, applied)
         for c in range(4):
             v0[c, fine_plane(halo), :] = 2.0 * near[c] - change[c]
 
-    def residual_fine(i):
-        total = [None] * 4
-        for s in range(2):
-            x = 2 * i + s
-            applied = mixed4(B0, [fine_stencil(v0, a0[x + 1], c, x + 2) for c in range(4)])
-            for c in range(4):
-                rest = f0[c, x] - applied[c]
-                total[c] = rest if s == 0 else total[c] + rest
-        for c in range(4):
-            r0[c, i] = total[c]
-
-    steps(x1, residual_fine)
+    steps(x1 - 2, lambda i: residual_fine(i + 1, 0, 8))
+    steps(x1 - 2, lambda i: residual_fine(i + 1, y0 - 8, 8))
+    steps(2, lambda i: residual_fine(i * (x1 - 1), 0, y0))
 
     for g in range(2):
         pieces = [
@@ -731,7 +750,7 @@
     double = pltpu.VMEM((2 * LANES, 2 * LANES), BF16)
     tall = pltpu.VMEM((2 * LANES, LANES), BF16)
     scratch = (
-        [vmem(2, 4, 2, y0, LANES), vmem(4, x0, y0, LANES), vmem(x0 + 2, y0, LANES)]
+        [vmem(2, 4, 2, y0, LANES), vmem(2, 4, x0, LANES), vmem(4, x0, y0, LANES), vmem(x0 + 2, y0, LANES)]
         + [vmem(4, (x0 + 4) * (y0 + 2 * PAD), LANES)] * 2
         + [vmem(2, 4, x0 + 2 * PAD, LANES)]
         + [vmem(4, x1, y0, LANES)]

time: 54.7 us -> 54.8 us (level)
  no operation moved by 1% of the time
where the time goes in v4:
time: 54.8 us; the launch traced here: 54.7 us
  Pallas kernels  53.7 us (98%)
  local copies, waits for them, and re-layouts  0.97 us (2%)
    pallas_call x1, Pallas kernels, per_device(): pl.pallas_call(functools.partial(kernel, nx, ny), out_shape=pltpu.VMEM(so...  53.7 us

profile of v4, /device:TPU:1, one launch (start us, length us, event | category | flops | bytes accessed | tf_op | source)
XLA Modules:
  0.0 54.7 jit_solution(12833489590771733066)
XLA Ops:
  0.0 53.7 %shard_map.73 = f32[4,16,32,128]{3,2,1,0:T(8,128)S(1)} custom-call(f32[4,16,32,128]{3,2,1,0:T(8,128)} %source.1, f32[16,32,128]{2,1,0:T(8,128)} %fine.1, f32[8,16,64]{2,1,0:T(8,128)} %second.1, f32[4,8,32]{2,1,0:T(8,128)} %third.1, f32[2,4,16]{2,1,0:T(4,128)} %coarse.1, f32[4,4,4]{2,1,0:T(4,128)} %mixers_in.1, f32[4,4,4]{2,1,0:T(4,128)} %smoothers_in.1), custom_call_target="tpu_custom_call" | custom-call | tf_op jit(solution)/shard_map/pallas_call | solution.py:788
  53.7 1.0 %copy.9 = f32[4,16,32,128]{3,2,1,0:T(8,128)} copy(f32[4,16,32,128]{3,2,1,0:T(8,128)S(1)} %shard_map.73) | data formatting | bytes 2097152

commit v5 on v4

--- a/solution.py
+++ b/solution.py
@@ -218,10 +218,10 @@
         return copies
 
     def exchange(g, s, p, packed, corner, cells, h, xs, ys):
-        own = pl.ds(PAD, ys)
+        own, held = pl.ds(PAD, ys), pl.ds(0, g.shape[0] - 1)
         copies = [
-            send(g.at[:, pl.ds(xs, h), own], g.at[:, pl.ds(0, h), own], (1, 0)),
-            send(g.at[:, pl.ds(h, h), own], g.at[:, pl.ds(xs + h, h), own], (-1, 0)),
+            send(g.at[held, pl.ds(xs, h), own], g.at[held, pl.ds(0, h), own], (1, 0)),
+            send(g.at[held, pl.ds(h, h), own], g.at[held, pl.ds(xs + h, h), own], (-1, 0)),
         ]
         copies += send_corners(s, packed, corner, cells, xs)
         copies.append(send(s.at[1], p.at[0], (0, 1)))
@@ -366,6 +366,15 @@
     coarse_copies = [send(t3, u3.at[0], (0, 1)), send(t3, u3.at[1], (0, -1))]
     g1[2, 3 : 3 + x1, PAD : PAD + y1, :] = jnp.concatenate([a1[...]] * 2, axis=-1)
     g2[1, 3 : 3 + x2, PAD : PAD + y2, :] = jnp.concatenate([a2[...]] * 4, axis=-1)
+    early = []
+    for g, xs, ys in ((g1, x1, y1), (g2, x2, y2)):
+        last, own = g.shape[0] - 1, pl.ds(PAD, ys)
+        early.append(
+            [
+                send(g.at[last, pl.ds(xs, 3), own], g.at[last, pl.ds(0, 3), own], (1, 0)),
+                send(g.at[last, pl.ds(3, 3), own], g.at[last, pl.ds(xs + 3, 3), own], (-1, 0)),
+            ]
+        )
     smooth1, mixer1 = smooth_matrix(1), mix_matrix(1)
     S1, B1, T1 = pair_rows(smooth1), pair_rows(mixer1), pair_rows(product(smooth1, mixer1))
     smooth2, mixer2 = smooth_matrix(2), mix_matrix(2)
@@ -511,7 +520,7 @@
             f0[c, x] = value - change[c]
 
     steps(x0, settle_fine)
-    unpack(copies, g1, p1, c1, cells1, planes1, 3, x1, y1)
+    unpack(copies + early[0], g1, p1, c1, cells1, planes1, 3, x1, y1)
 
     def relax_second(step):
         x = step + 1
@@ -561,7 +570,7 @@
             x1_part[c, step, row : row + rows, :] = value
 
     steps(x1 + 2, settle_second)
-    unpack(copies, g2, p2, c2, cells2, planes2, 3, x2, y2)
+    unpack(copies + early[1], g2, p2, c2, cells2, planes2, 3, x2, y2)
 
     def block_stencil(load, coefficient, x, xs, row, rows, segment):
         center = load(x, xs, row, rows)
@@ -776,7 +785,7 @@
         + [vmem(64, LANES)]
         + [tall, double, double, double, pltpu.VMEM((LANES, LANES), BF16), tall, tall]
     )
-    copies = 8 * 3 + 4 + 2 * 2 + (ny - 1) + 4 * 2
+    copies = 8 * 3 + 4 + 4 + 2 * 2 + (ny - 1) + 4 * 2
     scratch += [
         pltpu.SMEM(mixers.shape, F32),
         pltpu.SMEM(smoothers.shape, F32),

time: 54.8 us -> 54.7 us (level)
  no operation moved by 1% of the time
where the time goes in v5:
time: 54.7 us; the launch traced here: 54.6 us
  Pallas kernels  53.7 us (98%)
  local copies, waits for them, and re-layouts  0.97 us (2%)
    pallas_call x1, Pallas kernels, per_device(): pl.pallas_call(functools.partial(kernel, nx, ny), out_shape=pltpu.VMEM(so...  53.7 us

profile of v5, /device:TPU:1, one launch (start us, length us, event | category | flops | bytes accessed | tf_op | source)
XLA Modules:
  0.0 54.6 jit_solution(6163308892992781501)
XLA Ops:
  0.0 53.7 %shard_map.73 = f32[4,16,32,128]{3,2,1,0:T(8,128)S(1)} custom-call(f32[4,16,32,128]{3,2,1,0:T(8,128)} %source.1, f32[16,32,128]{2,1,0:T(8,128)} %fine.1, f32[8,16,64]{2,1,0:T(8,128)} %second.1, f32[4,8,32]{2,1,0:T(8,128)} %third.1, f32[2,4,16]{2,1,0:T(4,128)} %coarse.1, f32[4,4,4]{2,1,0:T(4,128)} %mixers_in.1, f32[4,4,4]{2,1,0:T(4,128)} %smoothers_in.1), custom_call_target="tpu_custom_call" | custom-call | tf_op jit(solution)/shard_map/pallas_call | solution.py:797
  53.7 1.0 %copy.9 = f32[4,16,32,128]{3,2,1,0:T(8,128)} copy(f32[4,16,32,128]{3,2,1,0:T(8,128)S(1)} %shard_map.73) | data formatting | bytes 2097152

commit v6 on v4

--- a/solution.py
+++ b/solution.py
@@ -263,7 +263,7 @@
             body(i)
             return carry
 
-        lax.fori_loop(0, count, step, 0)
+        lax.fori_loop(0, count, step, 0, unroll=2)
 
     def stencil_of(field, coefficient, c, x, row, rows, segment):
         center = field[c, x, row : row + rows, :]

time: 54.8 us -> 52.9 us (0.965)
  Pallas kernels: 53.7 us -> 51.8 us
    pallas_call x1, Pallas kernels: 53.7 us -> 51.8 us  [per_device(): pl.pallas_call(functools.partial(kernel, nx, ny), out_shape=pltpu.VMEM(so...]
where the time goes in v6:
time: 52.9 us; the launch traced here: 52.8 us
  Pallas kernels  51.8 us (98%)
  local copies, waits for them, and re-layouts  0.97 us (2%)
    pallas_call x1, Pallas kernels, per_device(): pl.pallas_call(functools.partial(kernel, nx, ny), out_shape=pltpu.VMEM(so...  51.8 us

profile of v6, /device:TPU:1, one launch (start us, length us, event | category | flops | bytes accessed | tf_op | source)
XLA Modules:
  0.0 52.8 jit_solution(8857510786682724030)
XLA Ops:
  0.0 51.8 %shard_map.73 = f32[4,16,32,128]{3,2,1,0:T(8,128)S(1)} custom-call(f32[4,16,32,128]{3,2,1,0:T(8,128)} %source.1, f32[16,32,128]{2,1,0:T(8,128)} %fine.1, f32[8,16,64]{2,1,0:T(8,128)} %second.1, f32[4,8,32]{2,1,0:T(8,128)} %third.1, f32[2,4,16]{2,1,0:T(4,128)} %coarse.1, f32[4,4,4]{2,1,0:T(4,128)} %mixers_in.1, f32[4,4,4]{2,1,0:T(4,128)} %smoothers_in.1), custom_call_target="tpu_custom_call" | custom-call | tf_op jit(solution)/shard_map/pallas_call | solution.py:788
  51.8 1.0 %copy.9 = f32[4,16,32,128]{3,2,1,0:T(8,128)} copy(f32[4,16,32,128]{3,2,1,0:T(8,128)S(1)} %shard_map.73) | data formatting | bytes 2097152
